TPU v7x, 512 devices: a whole 4x4x16 slice. The times are simulated.
512 devices in a mesh: pt: 64 (over y, z_hi, x), cen: 8 (over z_lo, core).
Axes of the slice: x: 4, y: 4, z: 16 (z_hi: 4, z_lo: 4; z = z_hi * 4 + z_lo), core: 2. Of those that a mesh axis runs over, the one named last changes fastest.
Arguments:
- points: float32 [32768, 1024], P('pt'), may hold values from -6 to 6
- centroids: float32 [2048, 1024], P('cen'), may hold values from -0.03125 to 0.03125
Outputs:
- final_centroids: float32 [8, 256, 1024], P('cen', 'pt')
- log_normaliser: float32 [32768], P('pt')
All inputs are finite; a program needn't handle non-finite values.
Results may differ from a plain program's by a relative error of at most 0.0014.
Values sent between devices are 32-bit elements; how exact they have to be, the bound alone decides.
No kernel may reach another device: no remote copies, remote signals or barrier semaphores. Data moves between devices by JAX's collectives and lax.ppermute only.
A program may use at most 64 MiB of HBM per device.

v0:
```python
import jax
import jax.numpy as jnp
from jax import lax
from jax.sharding import PartitionSpec as P

ITERS = 2


tau = 0.1


def score(points, rows):
    return (
        lax.dot_general(
            points,
            rows,
            (((1,), (1,)), ((), ())),
            precision=lax.Precision.HIGHEST,
            preferred_element_type=jnp.float32,
        )
        / tau
    )


def renormalise(weighted):
    return weighted / jnp.sqrt(jnp.sum(weighted * weighted, axis=1, keepdims=True) + 1e-06)


def shards(points, centroids):
    share = centroids.shape[0] // lax.axis_size("pt")
    current = centroids
    owned = centroids[:share]
    lognorm = jnp.zeros((points.shape[0],), jnp.float32)
    for turn in range(ITERS):
        logits = score(points, current)
        local_top = jnp.max(logits, axis=1)
        top = lax.pmax(local_top, "cen")
        expo = jnp.exp(logits - top[:, None])
        total = lax.psum(jnp.sum(expo, axis=1), "cen")
        resp = expo / total[:, None]
        lognorm = top + jnp.log(total)
        weighted = lax.dot_general(
            resp,
            points,
            (((0,), (0,)), ((), ())),
            precision=lax.Precision.HIGHEST,
            preferred_element_type=jnp.float32,
        )
        summed = lax.psum(weighted, "pt")
        current = renormalise(summed)
        start = lax.axis_index("pt") * share
        owned = lax.dynamic_slice_in_dim(current, start, share, 0)
    return (owned[None], lognorm)


def solution(mesh):
    return jax.shard_map(
        shards,
        mesh=mesh,
        in_specs=(P("pt", None), P("cen", None)),
        out_specs=(P("cen", "pt", None), P("pt")),
        check_vma=False,
    )
```

profile of v0, /device:TPU:4, one launch (start us, length us, event | category | flops | bytes accessed | tf_op | source)
XLA Modules:
  0.0 1775.8 jit_solution(4972693108405006190)
XLA Ops:
  7.2 0.0 copy-start
  7.2 0.0 all-reduce.3.cloned.1.call-start
  7.2 1.5 copy-done
  8.8 3.2 fusion.13
  12.0 17.6 pmax.14
  29.6 0.1 fusion.6
  29.7 13.6 psum.28
  43.3 3.0 fusion.4
  46.3 0.0 all-reduce.3.cloned.1.call-update
  46.3 0.0 all-reduce.5.cloned.1.call-start
  46.4 845.2 %all-reduce.3.cloned.1.call-done = f32[256,1024]{1,0:T(8,128)} async-done(((f32[256,1024]{1,0:T(8,128)}), f32[256,1024]{1,0:T(8,128)}) %all-reduce.3.cloned.1.call-update) | async-done | bytes 1048592 | tf_op jit(solution)/shard_map/psum | solution.py:49
  891.6 1.4 multiply_reduce_fusion.1
  893.0 3.2 fusion.14
  896.2 13.6 pmax.15
  909.8 0.1 fusion.7
  909.9 13.6 psum.30
  923.5 3.0 fusion.1
  926.4 0.0 all-reduce.5.cloned.1.call-update
  926.5 0.6 log_add_fusion
  927.1 839.0 %all-reduce.5.cloned.1.call-done = f32[256,1024]{1,0:T(8,128)} async-done(((f32[256,1024]{1,0:T(8,128)}), f32[256,1024]{1,0:T(8,128)}) %all-reduce.5.cloned.1.call-update) | async-done | bytes 1048592 | tf_op jit(solution)/shard_map/psum | solution.py:49
  1766.0 1.4 multiply_reduce_fusion
  1767.4 0.1 dynamic-slice
  1767.5 1.4 fusion.12
  (2 shorter events, 0.0 us)
Async XLA Ops:
  7.2 1.6 copy-start
  7.2 884.4 %all-reduce.3.cloned.1.call-start = ((), (), s32[]{:S(2)}) async-start(), calls=%async_computation | async-start | bytes 2097152 | tf_op jit(solution)/shard_map/psum | solution.py:49
  46.3 1719.7 %all-reduce.5.cloned.1.call-start = ((), (), s32[]{:S(2)}) async-start(), calls=%async_computation.1 | async-start | bytes 2097152 | tf_op jit(solution)/shard_map/psum | solution.py:49
Sparse Core Ops, SparseCore 0:
  46.4 845.1 all-reduce.2
  926.6 839.4 all-reduce.4
where the time goes:
time: 1780 us
  waiting for transfers between devices  1680 us (94%)
  blocking collectives  58.4 us (3%)
    psum x2, waiting for transfers between devices, shards(): summed = lax.psum(weighted, 'pt')  1680 us
  transfers between devices with their start and end apart: 2, of which 2 were waited for; matrix products, arithmetic and copies ran while one was open for 0% of the time, Pallas kernels for 0%

commit v1 on v0

v1 whole, which is shorter than its diff:
```python
import jax
import jax.numpy as jnp
from jax import lax
from jax.sharding import Mesh, PartitionSpec as P

ITERS = 2
TAU = 0.1
SIZES = {"y": 4, "zh": 4, "x": 4, "zl": 4, "core": 2}
PT = ("y", "zh", "x")
CEN = ("zl", "core")


def dot(a, b, dims):
    return lax.dot_general(
        a,
        b,
        (dims, ((), ())),
        precision=lax.Precision.HIGH,
        preferred_element_type=jnp.float32,
    )


def group_size(axes):
    n = 1
    for axis in axes:
        n *= lax.axis_size(axis)
    return n


def gather(block, axes):
    n = group_size(axes)
    copies = jnp.broadcast_to(block[None], (n,) + block.shape)
    return lax.all_to_all(copies, axes, split_axis=0, concat_axis=0, tiled=True)


def scatter_sum(rows, axes):
    n = group_size(axes)
    blocks = rows.reshape(n, rows.shape[0] // n, rows.shape[1])
    return jnp.sum(lax.all_to_all(blocks, axes, split_axis=0, concat_axis=0, tiled=True), axis=0)


def renormalise(weighted):
    return weighted / jnp.sqrt(jnp.sum(weighted * weighted, axis=1, keepdims=True) + 1e-06)


def shards(points, centroids):
    current = centroids
    for turn in range(ITERS):
        logits = dot(points, current, ((1,), (1,))) / TAU
        local_top = jnp.max(logits, axis=1)
        expo = jnp.exp(logits - local_top[:, None])
        both = gather(jnp.stack([local_top, jnp.sum(expo, axis=1)]), CEN)
        tops, sums = both[:, 0], both[:, 1]
        top = jnp.max(tops, axis=0)
        total = jnp.sum(sums * jnp.exp(tops - top), axis=0)
        resp = expo * (jnp.exp(local_top - top) / total)[:, None]
        weighted = dot(resp, points, ((0,), (0,)))
        if turn < ITERS - 1:
            part = scatter_sum(weighted, ("y", "x"))
            mine = renormalise(jnp.sum(gather(part, ("zh",)), axis=0))
            current = gather(mine, ("y", "x")).reshape(centroids.shape)
    owned = renormalise(scatter_sum(scatter_sum(weighted, ("y",)), ("zh", "x")))
    return owned[None], top + jnp.log(total)


def solution(mesh):
    fine = Mesh(mesh.devices.reshape(tuple(SIZES.values())), tuple(SIZES))
    return jax.shard_map(
        shards,
        mesh=fine,
        in_specs=(P(PT, None), P(CEN, None)),
        out_specs=(P(CEN, PT, None), P(PT)),
        check_vma=False,
    )
```

time: 1780 us -> 148 us (0.08)
  the two profiles are of different devices: /device:TPU:4 before, /device:TPU:32 now
where the time goes in v1:
time: 148 us; the launch traced here: 147 us
  blocking collectives  137 us (93%)
  matrix products  5.53 us (4%)
  other arithmetic  2.22 us (2%)
  local copies, waits for them, and re-layouts  1.83 us (1%)
    all_to_all x4, blocking collectives, gather(): return lax.all_to_all(copies, axes, split_axis=0, concat_axis=0, tiled=True)  72.6 us
    all_to_all x3, blocking collectives, scatter_sum(): lax.all_to_all(blocks, axes, split_axis=0, concat_axis=0, tiled=True)  64.3 us
    dot_general x4, matrix products, dot(): lax.dot_general(a, b, (dims, ((), ())), precision=lax.Precision.HIGH, pre...  5.53 us

profile of v1, /device:TPU:32, one launch (start us, length us, event | category | flops | bytes accessed | tf_op | source)
XLA Modules:
  0.0 147.1 jit_solution(11668045696031216740)
XLA Ops:
  0.6 0.0 copy-start
  0.6 1.6 %copy-done = f32[512,1024]{1,0:T(8,128)S(1)} copy-done((f32[512,1024]{1,0:T(8,128)S(1)}, f32[512,1024]{1,0:T(8,128)}, u32[]{:S(2)}) %copy-start) | copy-done | bytes 2097176
  2.2 2.3 %fusion.18 = (f32[512]{0:T(512)S(1)}, f32[512,256]{0,1:T(8,128)S(1)}) fusion(f32[512,1024]{1,0:T(8,128)S(1)} %copy-done, f32[256,1024]{1,0:T(8,128)} %param.3), kind=kOutput, calls=%fused_computation.37 | convolution fusion | flops 805568000 | bytes 3672064 | tf_op jit(solution)/shard_map/dot_general | solution.py:14
  4.5 0.1 fusion.4
  4.6 12.2 %all_to_all.35 = f32[8,2,512]{2,1,0:T(2,128)S(1)} all-to-all(f32[8,2,512]{2,1,0:T(2,128)S(1)} %broadcast_in_dim.8), channel_id=1, replica_groups=mesh['y'=4,'zh'=4,'x'=4,'zl'=4,'core'=2] {'zl','core'}, dimensions={0} | all-to-all | bytes 65536 | tf_op jit(solution)/shard_map/all_to_all | solution.py:33
  16.9 1.1 fusion.2
  18.0 21.9 %all_to_all.36 = f32[16,16,1024]{2,1,0:T(8,128)S(1)} all-to-all(f32[16,16,1024]{2,1,0:T(8,128)S(1)} %bitcast.40), channel_id=1, replica_groups=mesh['y'=4,'zh'=4,'x'=4,'zl'=4,'core'=2] {'y','x'}, dimensions={0} | all-to-all | bytes 2097152 | tf_op jit(solution)/shard_map/all_to_all | solution.py:39
  39.9 0.1 reduce_sum.94
  40.0 32.7 %all_to_all.37 = f32[4,16,1024]{2,1,0:T(8,128)S(1)} all-to-all(f32[4,16,1024]{2,1,0:T(8,128)S(1)} %broadcast_in_dim.9), channel_id=1, replica_groups=mesh['y'=4,'zh'=4,'x'=4,'zl'=4,'core'=2] {'zh'}, dimensions={0} | all-to-all | bytes 524288 | tf_op jit(solution)/shard_map/all_to_all | solution.py:33
  72.7 0.1 multiply_reduce_fusion
  72.9 0.1 broadcast_divide_fusion
  72.9 0.1 broadcast_in_dim.10
  73.1 20.2 %all_to_all.38 = f32[16,16,1024]{2,1,0:T(8,128)S(1)} all-to-all(f32[16,16,1024]{2,1,0:T(8,128)S(1)} %broadcast_in_dim.10), channel_id=1, replica_groups=mesh['y'=4,'zh'=4,'x'=4,'zl'=4,'core'=2] {'y','x'}, dimensions={0} | all-to-all | bytes 2097152 | tf_op jit(solution)/shard_map/all_to_all | solution.py:33
  93.2 1.1 fusion.19
  94.3 0.1 fusion.5
  94.5 7.5 %all_to_all.39 = f32[8,2,512]{2,1,0:T(2,128)S(1)} all-to-all(f32[8,2,512]{2,1,0:T(2,128)S(1)} %broadcast_in_dim.11), channel_id=1, replica_groups=mesh['y'=4,'zh'=4,'x'=4,'zl'=4,'core'=2] {'zl','core'}, dimensions={0} | all-to-all | bytes 65536 | tf_op jit(solution)/shard_map/all_to_all | solution.py:33
  102.0 0.6 log_add_fusion
  102.6 1.1 fusion
  103.7 17.7 %all_to_all.40 = f32[4,64,1024]{2,1,0:T(8,128)S(1)} all-to-all(f32[4,64,1024]{2,1,0:T(8,128)S(1)} %bitcast.41), channel_id=1, replica_groups=mesh['y'=4,'zh'=4,'x'=4,'zl'=4,'core'=2] {'y'}, dimensions={0} | all-to-all | bytes 2097152 | tf_op jit(solution)/shard_map/all_to_all | solution.py:39
  121.4 0.1 reduce_sum.99
  121.5 0.1 reshape.97
  121.6 24.7 %all_to_all.41 = f32[16,4,1024]{2,1,0:T(4,128)S(1)} all-to-all(f32[16,4,1024]{2,1,0:T(4,128)S(1)} %reshape.97), channel_id=1, replica_groups=mesh['y'=4,'zh'=4,'x'=4,'zl'=4,'core'=2] {'zh','x'}, dimensions={0} | all-to-all | bytes 524288 | tf_op jit(solution)/shard_map/all_to_all | solution.py:39
  146.3 0.1 reduce_sum.100
  146.3 0.1 multiply_reduce_fusion.1
  146.4 0.7 bitcast_divide_fusion
  (13 shorter events, 0.3 us)
Async XLA Ops:
  0.6 1.6 %copy-start = (f32[512,1024]{1,0:T(8,128)S(1)}, f32[512,1024]{1,0:T(8,128)}, u32[]{:S(2)}) copy-start(f32[512,1024]{1,0:T(8,128)} %param.2) | copy-start | bytes 6291460

commit v2 on v1

--- a/solution.py
+++ b/solution.py
@@ -3,7 +3,6 @@
 from jax import lax
 from jax.sharding import Mesh, PartitionSpec as P
 
-ITERS = 2
 TAU = 0.1
 SIZES = {"y": 4, "zh": 4, "x": 4, "zl": 4, "core": 2}
 PT = ("y", "zh", "x")
@@ -43,24 +42,43 @@
     return weighted / jnp.sqrt(jnp.sum(weighted * weighted, axis=1, keepdims=True) + 1e-06)
 
 
+def lse(values, axis):
+    top = jnp.max(values, axis=axis, keepdims=True)
+    expo = jnp.exp(values - top)
+    return jnp.squeeze(top, axis), expo, jnp.squeeze(top, axis) + jnp.log(jnp.sum(expo, axis=axis))
+
+
 def shards(points, centroids):
-    current = centroids
-    for turn in range(ITERS):
-        logits = dot(points, current, ((1,), (1,))) / TAU
-        local_top = jnp.max(logits, axis=1)
-        expo = jnp.exp(logits - local_top[:, None])
-        both = gather(jnp.stack([local_top, jnp.sum(expo, axis=1)]), CEN)
-        tops, sums = both[:, 0], both[:, 1]
-        top = jnp.max(tops, axis=0)
-        total = jnp.sum(sums * jnp.exp(tops - top), axis=0)
-        resp = expo * (jnp.exp(local_top - top) / total)[:, None]
-        weighted = dot(resp, points, ((0,), (0,)))
-        if turn < ITERS - 1:
-            part = scatter_sum(weighted, ("y", "x"))
-            mine = renormalise(jnp.sum(gather(part, ("zh",)), axis=0))
-            current = gather(mine, ("y", "x")).reshape(centroids.shape)
-    owned = renormalise(scatter_sum(scatter_sum(weighted, ("y",)), ("zh", "x")))
-    return owned[None], top + jnp.log(total)
+    half = points.shape[0] // 2
+    core = lax.axis_index("core")
+    share = lax.dynamic_slice_in_dim(points, core * half, half, 0)
+    first = lax.all_gather(share, "y", axis=0, tiled=True)
+
+    logits = dot(points, centroids, ((1,), (1,))) / TAU
+    top, expo, local = lse(logits, 1)
+    _, _, total = lse(gather(local, CEN), 0)
+    resp = expo * jnp.exp(top - total)[:, None]
+    weighted = dot(resp, points, ((0,), (0,)))
+    part = scatter_sum(weighted, ("y", "x"))
+    mine = renormalise(jnp.sum(gather(part, ("zh",)), axis=0))
+
+    other = lax.ppermute(first, "core", [(0, 1), (1, 0)])
+    current = gather(mine, ("x",)).reshape(-1, centroids.shape[1])
+    parts = []
+    for block in (first, other):
+        top, expo, local = lse(dot(block, current, ((1,), (1,))) / TAU, 1)
+        parts.append((top, expo, local))
+    local = jnp.stack([parts[0][2], parts[1][2]])
+    local = jnp.where(core == 0, local, local[::-1])
+    _, _, total = lse(gather(local, ("y",) + CEN), 0)
+    log_norm = lax.dynamic_slice_in_dim(total, lax.axis_index("y") * half, half, 1).reshape(-1)
+    total = jnp.where(core == 0, total, total[::-1])
+    weighted = 0.0
+    for i, block in enumerate((first, other)):
+        resp = parts[i][1] * jnp.exp(parts[i][0] - total[i])[:, None]
+        weighted += dot(resp, block, ((0,), (0,)))
+    owned = renormalise(scatter_sum(weighted, ("zh", "x")))
+    return owned[None], log_norm
 
 
 def solution(mesh):

time: 148 us -> 214 us (1.45)
  the two profiles are of different devices: /device:TPU:32 before, /device:TPU:1 now
where the time goes in v2:
time: 214 us; the launch traced here: 210 us
  waiting for transfers between devices  82 us (38%)
  blocking collectives  78.1 us (36%)
  matrix products  19.1 us (9%)
  between operations  14.3 us (7%)
  starting transfers between devices  9.55 us (4%)
  local copies, waits for them, and re-layouts  5.28 us (2%)
    all_gather x1, waiting for transfers between devices, shards(): first = lax.all_gather(share, 'y', axis=0, tiled=True)  59.3 us
    all_to_all x3, blocking collectives, gather(): return lax.all_to_all(copies, axes, split_axis=0, concat_axis=0, tiled=True)  56.5 us
    all_to_all x1, blocking collectives, scatter_sum(): lax.all_to_all(blocks, axes, split_axis=0, concat_axis=0, tiled=True)  21.6 us
    dot_general x6, matrix products, dot(): lax.dot_general(a, b, (dims, ((), ())), precision=lax.Precision.HIGH, pre...  19.1 us
    all_to_all x1, waiting for transfers between devices, scatter_sum(): lax.all_to_all(blocks, axes, split_axis=0, concat_axis=0, tiled=True)  17.2 us
    all_to_all x1, waiting for transfers between devices, gather(): return lax.all_to_all(copies, axes, split_axis=0, concat_axis=0, tiled=True)  5.49 us
  transfers between devices with their start and end apart: 4, of which 3 were waited for; matrix products, arithmetic and copies ran while one was open for 5% of the time, Pallas kernels for 0%

profile of v2, /device:TPU:1, one launch (start us, length us, event | category | flops | bytes accessed | tf_op | source)
XLA Modules:
  0.0 210.0 jit_solution(18328379173030188718)
XLA Ops:
  7.2 1.5 copy-done
  8.8 1.1 constant_dynamic-slice_fusion
  9.9 2.3 %fusion.19 = (f32[512]{0:T(512)S(1)}, f32[512,256]{0,1:T(8,128)S(1)}) fusion(f32[512,1024]{1,0:T(8,128)S(1)} %copy-done, f32[256,1024]{1,0:T(8,128)} %param.3), kind=kOutput, calls=%fused_computation.46 | convolution fusion | flops 805568000 | bytes 3672064 | tf_op jit(solution)/shard_map/dot_general | solution.py:13
  12.1 59.3 %all-gather.2.cloned.1.call-done = f32[1024,1024]{1,0:T(8,128)} async-done(((f32[256,1024]{1,0:T(8,128)}), f32[1024,1024]{1,0:T(8,128)}) %all-gather.2.cloned.1.call-update) | async-done | bytes 4194320 | tf_op jit(solution)/shard_map/all_gather | solution.py:55
  71.4 2.6 %collective-permute-start = (f32[1024,1024]{1,0:T(8,128)}, f32[1024,1024]{1,0:T(8,128)}, u32[]{:S(2)}, u32[]{:S(2)}) collective-permute-start(f32[1024,1024]{1,0:T(8,128)} %all-gather.2.cloned.1.call-done), channel_id=1, source_target_pairs={{0,1},{1,0},{2,3},{3,2},{4,5},{5,4},{6,7},{7,6},{8,9},{9,8},{10,11... | collective-permute-start | bytes 12582920 | tf_op jit(solution)/shard_map/ppermute | solution.py:65
  74.0 0.1 fusion.2
  74.1 9.6 %all_to_all.34 = f32[8,1,512]{2,1,0:T(1,128)S(1)} all-to-all(f32[8,1,512]{2,1,0:T(1,128)S(1)} %broadcast_in_dim.8), channel_id=1, replica_groups=mesh['y'=4,'zh'=4,'x'=4,'zl'=4,'core'=2] {'zl','core'}, dimensions={0} | all-to-all | bytes 32768 | tf_op jit(solution)/shard_map/all_to_all | solution.py:32
  83.9 1.1 fusion
  84.9 21.6 %all_to_all.35 = f32[16,16,1024]{2,1,0:T(8,128)S(1)} all-to-all(f32[16,16,1024]{2,1,0:T(8,128)S(1)} %bitcast.26), channel_id=1, replica_groups=mesh['y'=4,'zh'=4,'x'=4,'zl'=4,'core'=2] {'y','x'}, dimensions={0} | all-to-all | bytes 2097152 | tf_op jit(solution)/shard_map/all_to_all | solution.py:38
  106.5 0.1 reduce_sum.94
  106.6 26.3 %all_to_all.36 = f32[4,16,1024]{2,1,0:T(8,128)S(1)} all-to-all(f32[4,16,1024]{2,1,0:T(8,128)S(1)} %broadcast_in_dim.9), channel_id=1, replica_groups=mesh['y'=4,'zh'=4,'x'=4,'zl'=4,'core'=2] {'zh'}, dimensions={0} | all-to-all | bytes 524288 | tf_op jit(solution)/shard_map/all_to_all | solution.py:32
  132.9 0.1 multiply_reduce_fusion
  133.1 0.1 broadcast_divide_fusion
  133.2 0.7 broadcast_in_dim.10
  133.9 3.4 %all-to-all-start.3 = ((f32[4,16,1024]{2,1,0:T(8,128)}), f32[4,16,1024]{2,1,0:T(8,128)S(1)}, u32[]{:S(2)}, u32[]{:S(2)}) async-start(f32[4,16,1024]{2,1,0:T(8,128)} %broadcast_in_dim.10), calls=%async_computation.3 | async-start | bytes 524288 | tf_op jit(solution)/shard_map/all_to_all | solution.py:32
  137.3 5.5 %all-to-all-done.3 = f32[4,16,1024]{2,1,0:T(8,128)S(1)} async-done(((f32[4,16,1024]{2,1,0:T(8,128)}), f32[4,16,1024]{2,1,0:T(8,128)S(1)}, u32[]{:S(2)}, u32[]{:S(2)}) %all-to-all-start.3) | async-done | bytes 262176 | tf_op jit(solution)/shard_map/all_to_all | solution.py:32
  142.8 4.2 %fusion.20 = (f32[1024]{0:T(1024)S(1)}, f32[1024,64]{0,1:T(8,128)S(1)}) fusion(f32[1024,1024]{1,0:T(8,128)} %all-gather.2.cloned.1.call-done, f32[64,1024]{1,0:T(8,128)S(1)} %bitcast.27), kind=kOutput, calls=%fused_computation.47 | convolution fusion | flops 402783232 | bytes 4722688 | tf_op jit(solution)/shard_map/dot_general | solution.py:13
  147.1 4.2 %fusion.21 = (f32[1024]{0:T(1024)S(1)}, f32[1024,64]{0,1:T(8,128)S(1)}) fusion(f32[1024,1024]{1,0:T(8,128)} %collective-permute-done, f32[64,1024]{1,0:T(8,128)S(1)} %bitcast.28), kind=kOutput, calls=%fused_computation.48 | convolution fusion | flops 402783232 | bytes 4722688 | tf_op jit(solution)/shard_map/dot_general | solution.py:13
  151.4 0.2 rev.6
  151.7 0.1 broadcast_in_dim.11
  151.8 20.6 %all_to_all.37 = f32[32,2,1024]{2,1,0:T(2,128)S(1)} all-to-all(f32[32,2,1024]{2,1,0:T(2,128)S(1)} %broadcast_in_dim.11), channel_id=1, replica_groups=mesh['y'=4,'zh'=4,'x'=4,'zl'=4,'core'=2] {'y','zl','core'}, dimensions={0} | all-to-all | bytes 524288 | tf_op jit(solution)/shard_map/all_to_all | solution.py:32
  172.3 0.1 reduce_max.49
  172.4 0.1 fusion.4
  172.6 0.2 rev.7
  172.9 3.6 %fusion.6 = f32[64,1024]{1,0:T(8,128)S(1)} fusion(f32[1024,1024]{1,0:T(8,128)} %all-gather.2.cloned.1.call-done, f32[1024,64]{0,1:T(8,128)S(1)} %get-tuple-element.7, f32[1024]{0:T(1024)S(1)} %subtract_exponential_fusion.7, f32[1024]{0:T(1024)S(1)} %get-tuple-element.6), kind=kOutput, calls=%fused_computation.12 | convolution fusion | flops 402784256 | bytes 4726784 | tf_op jit(solution)/shard_map/dot_general | solution.py:13
  176.5 3.6 %convolution_add_fusion = f32[64,1024]{1,0:T(8,128)S(1)} fusion(f32[64,1024]{1,0:T(8,128)S(1)} %fusion.6, f32[1024,1024]{1,0:T(8,128)} %collective-permute-done, f32[1024,64]{0,1:T(8,128)S(1)} %get-tuple-element.9, f32[1024]{0:T(1024)S(1)} %subtract_exponential_fusion.6, f32[1024]{0:T(1024)S(1)} %get-tuple-element.8), kind=kOutput, calls=%fused_computation.1 | convolution fusion | flops 402849792 | bytes 4988928 | tf_op jit(solution)/shard_map/dot_general | solution.py:13
  180.1 0.8 reshape.148
  180.9 3.5 %all-to-all-start.5 = ((f32[16,4,1024]{2,1,0:T(4,128)}), f32[16,4,1024]{2,1,0:T(4,128)S(1)}, u32[]{:S(2)}, u32[]{:S(2)}) async-start(f32[16,4,1024]{2,1,0:T(4,128)} %reshape.148), calls=%async_computation.5 | async-start | bytes 524288 | tf_op jit(solution)/shard_map/all_to_all | solution.py:38
  184.5 0.6 copy.13
  185.0 17.2 %all-to-all-done.5 = f32[16,4,1024]{2,1,0:T(4,128)S(1)} async-done(((f32[16,4,1024]{2,1,0:T(4,128)}), f32[16,4,1024]{2,1,0:T(4,128)S(1)}, u32[]{:S(2)}, u32[]{:S(2)}) %all-to-all-start.5) | async-done | bytes 262176 | tf_op jit(solution)/shard_map/all_to_all | solution.py:38
  202.3 0.1 multiply_reduce_fusion.1
  202.5 0.7 bitcast_divide_fusion
  (26 shorter events, 0.5 us)
Async XLA Ops:
  7.2 1.6 copy-start
  7.2 64.2 %all-gather.2.cloned.1.call-start = ((), (), s32[]{:S(2)}) async-start(), calls=%async_computation.6 | async-start | bytes 5242880 | tf_op jit(solution)/shard_map/all_gather | solution.py:55
  71.4 75.7 %collective-permute-start = (f32[1024,1024]{1,0:T(8,128)}, f32[1024,1024]{1,0:T(8,128)}, u32[]{:S(2)}, u32[]{:S(2)}) collective-permute-start(f32[1024,1024]{1,0:T(8,128)} %all-gather.2.cloned.1.call-done), channel_id=1, source_target_pairs={{0,1},{1,0},{2,3},{3,2},{4,5},{5,4},{6,7},{7,6},{8,9},{9,8},{10,11... | collective-permute-start | bytes 12582920 | tf_op jit(solution)/shard_map/ppermute | solution.py:65
  133.9 8.9 %all-to-all-start.3 = ((f32[4,16,1024]{2,1,0:T(8,128)}), f32[4,16,1024]{2,1,0:T(8,128)S(1)}, u32[]{:S(2)}, u32[]{:S(2)}) async-start(f32[4,16,1024]{2,1,0:T(8,128)} %broadcast_in_dim.10), calls=%async_computation.3 | async-start | bytes 524288 | tf_op jit(solution)/shard_map/all_to_all | solution.py:32
  180.9 21.4 %all-to-all-start.5 = ((f32[16,4,1024]{2,1,0:T(4,128)}), f32[16,4,1024]{2,1,0:T(4,128)S(1)}, u32[]{:S(2)}, u32[]{:S(2)}) async-start(f32[16,4,1024]{2,1,0:T(4,128)} %reshape.148), calls=%async_computation.5 | async-start | bytes 524288 | tf_op jit(solution)/shard_map/all_to_all | solution.py:38
Sparse Core Ops, SparseCore 0:
  10.1 61.2 all-gather.1

commit v3 on v2

--- a/solution.py
+++ b/solution.py
@@ -52,7 +52,7 @@
     half = points.shape[0] // 2
     core = lax.axis_index("core")
     share = lax.dynamic_slice_in_dim(points, core * half, half, 0)
-    first = lax.all_gather(share, "y", axis=0, tiled=True)
+    ring = lax.all_gather(share, "y", axis=0, tiled=True)
 
     logits = dot(points, centroids, ((1,), (1,))) / TAU
     top, expo, local = lse(logits, 1)
@@ -62,22 +62,15 @@
     part = scatter_sum(weighted, ("y", "x"))
     mine = renormalise(jnp.sum(gather(part, ("zh",)), axis=0))
 
-    other = lax.ppermute(first, "core", [(0, 1), (1, 0)])
-    current = gather(mine, ("x",)).reshape(-1, centroids.shape[1])
-    parts = []
-    for block in (first, other):
-        top, expo, local = lse(dot(block, current, ((1,), (1,))) / TAU, 1)
-        parts.append((top, expo, local))
-    local = jnp.stack([parts[0][2], parts[1][2]])
-    local = jnp.where(core == 0, local, local[::-1])
-    _, _, total = lse(gather(local, ("y",) + CEN), 0)
-    log_norm = lax.dynamic_slice_in_dim(total, lax.axis_index("y") * half, half, 1).reshape(-1)
-    total = jnp.where(core == 0, total, total[::-1])
-    weighted = 0.0
-    for i, block in enumerate((first, other)):
-        resp = parts[i][1] * jnp.exp(parts[i][0] - total[i])[:, None]
-        weighted += dot(resp, block, ((0,), (0,)))
-    owned = renormalise(scatter_sum(weighted, ("zh", "x")))
+    current = gather(mine, ("core", "x")).reshape(-1, centroids.shape[1])
+    top, expo, local = lse(dot(ring, current, ((1,), (1,))) / TAU, 1)
+    _, _, total = lse(gather(local, ("y", "zl")), 0)
+    here = lax.dynamic_slice_in_dim(total, lax.axis_index("y") * half, half, 0)
+    there = lax.ppermute(here, "core", [(0, 1), (1, 0)])
+    log_norm = jnp.where(core == 0, jnp.concatenate([here, there]), jnp.concatenate([there, here]))
+    resp = expo * jnp.exp(top - total)[:, None]
+    weighted = dot(resp, ring, ((0,), (0,)))
+    owned = renormalise(scatter_sum(scatter_sum(weighted, ("core",)), ("zh", "x")))
     return owned[None], log_norm
 
 

time: 214 us -> 153 us (0.71)
  waiting for transfers between devices: 82 us -> 15.1 us
  blocking collectives: 78.1 us -> 98 us
  matrix products: 19.1 us -> 11.3 us
  starting transfers between devices: 9.55 us -> 5.87 us
    all_gather x1, waiting for transfers between devices: 59.3 us -> 0.01 us  [shards(): ring = lax.all_gather(share, 'y', axis=0, tiled=True)]
    all_to_all x3 -> x4, blocking collectives: 56.5 us -> 71.8 us  [gather(): return lax.all_to_all(copies, axes, split_axis=0, concat_axis=0, tiled=True)]
    dot_general x6 -> x4, matrix products: 19.1 us -> 11.3 us  [dot(): lax.dot_general(a, b, (dims, ((), ())), precision=lax.Precision.HIGH, pre...]
    all_to_all x1 -> x0, waiting for transfers between devices: 5.49 us -> none  [gather(): return lax.all_to_all(copies, axes, split_axis=0, concat_axis=0, tiled=True)]
    all_to_all x1 -> x2, blocking collectives: 21.6 us -> 26.2 us  [scatter_sum(): lax.all_to_all(blocks, axes, split_axis=0, concat_axis=0, tiled=True)]
    all_to_all x1 -> x0, starting transfers between devices: 3.4 us -> none  [gather(): return lax.all_to_all(copies, axes, split_axis=0, concat_axis=0, tiled=True)]
    all_to_all x1, waiting for transfers between devices: 17.2 us -> 14.3 us  [scatter_sum(): lax.all_to_all(blocks, axes, split_axis=0, concat_axis=0, tiled=True)]
  transfers between devices with their start and end apart: 4 -> 3, of which waited for: 3 -> 2; matrix products, arithmetic and copies ran while one was open for 5% -> 3% of each run, Pallas kernels for 0% -> 0%
where the time goes in v3:
time: 153 us; the launch traced here: 150 us
  blocking collectives  98 us (64%)
  waiting for transfers between devices  15.1 us (10%)
  between operations  14.2 us (9%)
  matrix products  11.3 us (7%)
  starting transfers between devices  5.87 us (4%)
  local copies, waits for them, and re-layouts  3.59 us (2%)
  other arithmetic  2.16 us (1%)
    all_to_all x4, blocking collectives, gather(): return lax.all_to_all(copies, axes, split_axis=0, concat_axis=0, tiled=True)  71.8 us
    all_to_all x2, blocking collectives, scatter_sum(): lax.all_to_all(blocks, axes, split_axis=0, concat_axis=0, tiled=True)  26.2 us
    all_to_all x1, waiting for transfers between devices, scatter_sum(): lax.all_to_all(blocks, axes, split_axis=0, concat_axis=0, tiled=True)  14.3 us
    dot_general x4, matrix products, dot(): lax.dot_general(a, b, (dims, ((), ())), precision=lax.Precision.HIGH, pre...  11.3 us
    all_to_all x1, starting transfers between devices, scatter_sum(): lax.all_to_all(blocks, axes, split_axis=0, concat_axis=0, tiled=True)  3.53 us
  transfers between devices with their start and end apart: 3, of which 2 were waited for; matrix products, arithmetic and copies ran while one was open for 3% of the time, Pallas kernels for 0%

profile of v3, /device:TPU:1, one launch (start us, length us, event | category | flops | bytes accessed | tf_op | source)
XLA Modules:
  0.0 150.1 jit_solution(3257145287132780289)
XLA Ops:
  7.2 0.0 copy-start
  7.2 0.0 all-gather.2.cloned.1.call-start
  7.2 1.5 %copy-done = f32[512,1024]{1,0:T(8,128)S(1)} copy-done((f32[512,1024]{1,0:T(8,128)S(1)}, f32[512,1024]{1,0:T(8,128)}, u32[]{:S(2)}) %copy-start) | copy-done | bytes 2097176
  8.8 1.1 constant_dynamic-slice_fusion
  9.8 0.0 all-gather.2.cloned.1.call-update
  9.9 2.3 %fusion.14 = (f32[512]{0:T(512)S(1)}, f32[512,256]{0,1:T(8,128)S(1)}) fusion(f32[512,1024]{1,0:T(8,128)S(1)} %copy-done, f32[256,1024]{1,0:T(8,128)} %param.3), kind=kOutput, calls=%fused_computation.33 | convolution fusion | flops 805568000 | bytes 3672064 | tf_op jit(solution)/shard_map/dot_general | solution.py:13
  12.1 0.1 fusion.4
  12.3 14.2 %all_to_all.43 = f32[8,1,512]{2,1,0:T(1,128)S(1)} all-to-all(f32[8,1,512]{2,1,0:T(1,128)S(1)} %broadcast_in_dim.8), channel_id=1, replica_groups=mesh['y'=4,'zh'=4,'x'=4,'zl'=4,'core'=2] {'zl','core'}, dimensions={0} | all-to-all | bytes 32768 | tf_op jit(solution)/shard_map/all_to_all | solution.py:32
  26.5 1.1 fusion.2
  27.6 20.7 %all_to_all.44 = f32[16,16,1024]{2,1,0:T(8,128)S(1)} all-to-all(f32[16,16,1024]{2,1,0:T(8,128)S(1)} %bitcast.23), channel_id=1, replica_groups=mesh['y'=4,'zh'=4,'x'=4,'zl'=4,'core'=2] {'y','x'}, dimensions={0} | all-to-all | bytes 2097152 | tf_op jit(solution)/shard_map/all_to_all | solution.py:38
  48.3 0.1 reduce_sum.94
  48.4 29.0 %all_to_all.45 = f32[4,16,1024]{2,1,0:T(8,128)S(1)} all-to-all(f32[4,16,1024]{2,1,0:T(8,128)S(1)} %broadcast_in_dim.9), channel_id=1, replica_groups=mesh['y'=4,'zh'=4,'x'=4,'zl'=4,'core'=2] {'zh'}, dimensions={0} | all-to-all | bytes 524288 | tf_op jit(solution)/shard_map/all_to_all | solution.py:32
  77.4 0.1 multiply_reduce_fusion
  77.6 0.1 broadcast_divide_fusion
  77.7 0.1 broadcast_in_dim.10
  77.7 17.3 %all_to_all.46 = f32[8,16,1024]{2,1,0:T(8,128)S(1)} all-to-all(f32[8,16,1024]{2,1,0:T(8,128)S(1)} %broadcast_in_dim.10), channel_id=1, replica_groups=mesh['y'=4,'zh'=4,'x'=4,'zl'=4,'core'=2] {'core','x'}, dimensions={0} | all-to-all | bytes 1048576 | tf_op jit(solution)/shard_map/all_to_all | solution.py:32
  95.0 4.4 %fusion.15 = (f32[1024]{0:T(1024)S(1)}, f32[1024,128]{0,1:T(8,128)S(1)}) fusion(f32[1024,1024]{1,0:T(8,128)} %all-gather.2.cloned.1.call-done, f32[128,1024]{1,0:T(8,128)S(1)} %bitcast.24), kind=kOutput, calls=%fused_computation.34 | convolution fusion | flops 805567488 | bytes 5246976 | tf_op jit(solution)/shard_map/dot_general | solution.py:13
  99.4 0.1 fusion.5
  99.5 11.4 %all_to_all.47 = f32[16,1,1024]{2,1,0:T(1,128)S(1)} all-to-all(f32[16,1,1024]{2,1,0:T(1,128)S(1)} %broadcast_in_dim.11), channel_id=1, replica_groups=mesh['y'=4,'zh'=4,'x'=4,'zl'=4,'core'=2] {'y','zl'}, dimensions={0} | all-to-all | bytes 131072 | tf_op jit(solution)/shard_map/all_to_all | solution.py:32
  110.9 0.1 reduce_max.39
  111.0 3.5 %fusion = f32[128,1024]{1,0:T(8,128)S(1)} fusion(f32[1024,1024]{1,0:T(8,128)} %all-gather.2.cloned.1.call-done, f32[1024,128]{0,1:T(8,128)S(1)} %get-tuple-element.7, f32[1024]{0:T(1024)S(1)} %get-tuple-element.2, f32[1024]{0:T(1024)S(1)} %get-tuple-element.6), kind=kOutput, calls=%fused_computation.2 | convolution fusion | flops 805568512 | bytes 5251072 | tf_op jit(solution)/shard_map/dot_general | solution.py:13
  114.6 5.5 %all_to_all.48 = f32[2,64,1024]{2,1,0:T(8,128)S(1)} all-to-all(f32[2,64,1024]{2,1,0:T(8,128)S(1)} %bitcast.25), channel_id=1, replica_groups=mesh['y'=4,'zh'=4,'x'=4,'zl'=4,'core'=2] {'core'}, dimensions={0} | all-to-all | bytes 1048576 | tf_op jit(solution)/shard_map/all_to_all | solution.py:38
  120.1 0.8 reshape.121
  120.8 3.5 %all-to-all-start.6 = ((f32[16,4,1024]{2,1,0:T(4,128)}), f32[16,4,1024]{2,1,0:T(4,128)S(1)}, u32[]{:S(2)}, u32[]{:S(2)}) async-start(f32[16,4,1024]{2,1,0:T(4,128)} %reshape.121), calls=%async_computation.6 | async-start | bytes 524288 | tf_op jit(solution)/shard_map/all_to_all | solution.py:38
  124.4 0.1 dynamic_slice.7
  124.5 2.3 %collective-permute-start = (f32[256]{0:T(256)S(1)}, f32[256]{0:T(256)S(1)}, u32[]{:S(2)}, u32[]{:S(2)}) collective-permute-start(f32[256]{0:T(256)S(1)} %dynamic_slice.7), channel_id=1, source_target_pairs={{0,1},{1,0},{2,3},{3,2},{4,5},{5,4},{6,7},{7,6},{8,9},{9,8},{10,11... | collective-permute-start | bytes 3080 | tf_op jit(solution)/shard_map/ppermute | solution.py:69
  126.8 0.8 collective-permute-done
  127.6 0.6 maximum_select_fusion
  128.2 14.3 %all-to-all-done.6 = f32[16,4,1024]{2,1,0:T(4,128)S(1)} async-done(((f32[16,4,1024]{2,1,0:T(4,128)}), f32[16,4,1024]{2,1,0:T(4,128)S(1)}, u32[]{:S(2)}, u32[]{:S(2)}) %all-to-all-start.6) | async-done | bytes 262176 | tf_op jit(solution)/shard_map/all_to_all | solution.py:38
  142.4 0.1 reduce_sum.100
  142.5 0.1 multiply_reduce_fusion.1
  142.6 0.7 bitcast_divide_fusion
  (15 shorter events, 0.3 us)
Async XLA Ops:
  7.2 1.6 %copy-start = (f32[512,1024]{1,0:T(8,128)S(1)}, f32[512,1024]{1,0:T(8,128)}, u32[]{:S(2)}) copy-start(f32[512,1024]{1,0:T(8,128)} %param.2) | copy-start | bytes 6291460
  7.2 87.8 %all-gather.2.cloned.1.call-start = ((), (), s32[]{:S(2)}) async-start(), calls=%async_computation.7 | async-start | bytes 5242880 | tf_op jit(solution)/shard_map/all_gather | solution.py:55
  120.8 21.6 %all-to-all-start.6 = ((f32[16,4,1024]{2,1,0:T(4,128)}), f32[16,4,1024]{2,1,0:T(4,128)S(1)}, u32[]{:S(2)}, u32[]{:S(2)}) async-start(f32[16,4,1024]{2,1,0:T(4,128)} %reshape.121), calls=%async_computation.6 | async-start | bytes 524288 | tf_op jit(solution)/shard_map/all_to_all | solution.py:38
  124.5 3.1 %collective-permute-start = (f32[256]{0:T(256)S(1)}, f32[256]{0:T(256)S(1)}, u32[]{:S(2)}, u32[]{:S(2)}) collective-permute-start(f32[256]{0:T(256)S(1)} %dynamic_slice.7), channel_id=1, source_target_pairs={{0,1},{1,0},{2,3},{3,2},{4,5},{5,4},{6,7},{7,6},{8,9},{9,8},{10,11... | collective-permute-start | bytes 3080 | tf_op jit(solution)/shard_map/ppermute | solution.py:69
Sparse Core Ops, SparseCore 0:
  10.1 71.5 all-gather.1

commit v4 on v1

--- a/solution.py
+++ b/solution.py
@@ -43,24 +43,27 @@
     return weighted / jnp.sqrt(jnp.sum(weighted * weighted, axis=1, keepdims=True) + 1e-06)
 
 
+def lse(values, axis):
+    top = jnp.max(values, axis=axis, keepdims=True)
+    expo = jnp.exp(values - top)
+    return jnp.squeeze(top, axis), expo, jnp.squeeze(top, axis) + jnp.log(jnp.sum(expo, axis=axis))
+
+
 def shards(points, centroids):
-    current = centroids
+    split = tuple(lax.axis_size(axis) for axis in PT)
+    current = centroids.reshape(split + (-1, centroids.shape[1])).swapaxes(1, 2).reshape(centroids.shape)
     for turn in range(ITERS):
         logits = dot(points, current, ((1,), (1,))) / TAU
-        local_top = jnp.max(logits, axis=1)
-        expo = jnp.exp(logits - local_top[:, None])
-        both = gather(jnp.stack([local_top, jnp.sum(expo, axis=1)]), CEN)
-        tops, sums = both[:, 0], both[:, 1]
-        top = jnp.max(tops, axis=0)
-        total = jnp.sum(sums * jnp.exp(tops - top), axis=0)
-        resp = expo * (jnp.exp(local_top - top) / total)[:, None]
+        top, expo, local = lse(logits, 1)
+        _, _, total = lse(gather(local, CEN), 0)
+        resp = expo * jnp.exp(top - total)[:, None]
         weighted = dot(resp, points, ((0,), (0,)))
+        part = scatter_sum(weighted, ("y", "x"))
         if turn < ITERS - 1:
-            part = scatter_sum(weighted, ("y", "x"))
             mine = renormalise(jnp.sum(gather(part, ("zh",)), axis=0))
             current = gather(mine, ("y", "x")).reshape(centroids.shape)
-    owned = renormalise(scatter_sum(scatter_sum(weighted, ("y",)), ("zh", "x")))
-    return owned[None], top + jnp.log(total)
+    owned = renormalise(scatter_sum(part, ("zh",)))
+    return owned[None], total
 
 
 def solution(mesh):

time: 148 us -> 145 us (0.980)
  the two profiles are of different devices: /device:TPU:32 before, /device:TPU:1 now
where the time goes in v4:
time: 145 us; the launch traced here: 144 us
  blocking collectives  130 us (90%)
  local copies, waits for them, and re-layouts  5.53 us (4%)
  matrix products  5.51 us (4%)
  other arithmetic  2.13 us (1%)
    all_to_all x4, blocking collectives, gather(): return lax.all_to_all(copies, axes, split_axis=0, concat_axis=0, tiled=True)  75.7 us
    all_to_all x3, blocking collectives, scatter_sum(): lax.all_to_all(blocks, axes, split_axis=0, concat_axis=0, tiled=True)  54.5 us
    dot_general x4, matrix products, dot(): lax.dot_general(a, b, (dims, ((), ())), precision=lax.Precision.HIGH, pre...  5.51 us
    reshape x3, local copies, waits for them, and re-layouts, shards(): centroids.reshape(split + (-1, centroids.shape[1])).swapaxes(1, 2)  5.33 us

profile of v4, /device:TPU:1, one launch (start us, length us, event | category | flops | bytes accessed | tf_op | source)
XLA Modules:
  0.0 144.1 jit_solution(9969244952485478286)
XLA Ops:
  0.6 0.0 copy-start
  0.6 2.7 %reshape.124 = f32[4,4,4,4,1024]{4,3,2,1,0:T(4,128)} reshape(f32[256,1024]{1,0:T(8,128)} %param.3) | data formatting | bytes 2097152 | tf_op jit(solution)/shard_map/reshape | solution.py:54
  3.3 1.3 copy.16
  4.6 1.4 reshape.125
  6.0 0.0 copy-done
  6.0 2.3 %fusion.14 = (f32[512]{0:T(512)S(1)}, f32[512,256]{0,1:T(8,128)S(1)}) fusion(f32[512,1024]{1,0:T(8,128)S(1)} %copy-done, f32[256,1024]{1,0:T(8,128)} %reshape.125), kind=kOutput, calls=%fused_computation.32 | convolution fusion | flops 805568000 | bytes 3672064 | tf_op jit(solution)/shard_map/dot_general | solution.py:14
  8.3 0.1 fusion.4
  8.4 14.2 %all_to_all.43 = f32[8,1,512]{2,1,0:T(1,128)S(1)} all-to-all(f32[8,1,512]{2,1,0:T(1,128)S(1)} %broadcast_in_dim.8), channel_id=1, replica_groups=mesh['y'=4,'zh'=4,'x'=4,'zl'=4,'core'=2] {'zl','core'}, dimensions={0} | all-to-all | bytes 32768 | tf_op jit(solution)/shard_map/all_to_all | solution.py:33
  22.6 1.1 fusion.2
  23.7 20.7 %all_to_all.44 = f32[16,16,1024]{2,1,0:T(8,128)S(1)} all-to-all(f32[16,16,1024]{2,1,0:T(8,128)S(1)} %bitcast.28), channel_id=1, replica_groups=mesh['y'=4,'zh'=4,'x'=4,'zl'=4,'core'=2] {'y','x'}, dimensions={0} | all-to-all | bytes 2097152 | tf_op jit(solution)/shard_map/all_to_all | solution.py:39
  44.4 0.1 reduce_sum.94
  44.5 28.9 %all_to_all.45 = f32[4,16,1024]{2,1,0:T(8,128)S(1)} all-to-all(f32[4,16,1024]{2,1,0:T(8,128)S(1)} %broadcast_in_dim.9), channel_id=1, replica_groups=mesh['y'=4,'zh'=4,'x'=4,'zl'=4,'core'=2] {'zh'}, dimensions={0} | all-to-all | bytes 524288 | tf_op jit(solution)/shard_map/all_to_all | solution.py:33
  73.4 0.1 multiply_reduce_fusion
  73.5 0.1 broadcast_divide_fusion
  73.6 0.1 broadcast_in_dim.10
  73.8 16.0 %all_to_all.46 = f32[16,16,1024]{2,1,0:T(8,128)S(1)} all-to-all(f32[16,16,1024]{2,1,0:T(8,128)S(1)} %broadcast_in_dim.10), channel_id=1, replica_groups=mesh['y'=4,'zh'=4,'x'=4,'zl'=4,'core'=2] {'y','x'}, dimensions={0} | all-to-all | bytes 2097152 | tf_op jit(solution)/shard_map/all_to_all | solution.py:33
  89.8 1.1 fusion.15
  90.9 0.1 fusion.5
  91.0 16.6 %all_to_all.47 = f32[8,1,512]{2,1,0:T(1,128)S(1)} all-to-all(f32[8,1,512]{2,1,0:T(1,128)S(1)} %broadcast_in_dim.11), channel_id=1, replica_groups=mesh['y'=4,'zh'=4,'x'=4,'zl'=4,'core'=2] {'zl','core'}, dimensions={0} | all-to-all | bytes 32768 | tf_op jit(solution)/shard_map/all_to_all | solution.py:33
  107.7 0.6 subtract_exponential_fusion.4
  108.3 1.1 fusion
  109.4 18.9 %all_to_all.48 = f32[16,16,1024]{2,1,0:T(8,128)S(1)} all-to-all(f32[16,16,1024]{2,1,0:T(8,128)S(1)} %bitcast.29), channel_id=1, replica_groups=mesh['y'=4,'zh'=4,'x'=4,'zl'=4,'core'=2] {'y','x'}, dimensions={0} | all-to-all | bytes 2097152 | tf_op jit(solution)/shard_map/all_to_all | solution.py:39
  128.3 0.1 reduce_sum.99
  128.4 14.9 %all_to_all.49 = f32[4,4,1024]{2,1,0:T(4,128)S(1)} all-to-all(f32[4,4,1024]{2,1,0:T(4,128)S(1)} %reshape.129), channel_id=1, replica_groups=mesh['y'=4,'zh'=4,'x'=4,'zl'=4,'core'=2] {'zh'}, dimensions={0} | all-to-all | bytes 131072 | tf_op jit(solution)/shard_map/all_to_all | solution.py:39
  143.3 0.1 multiply_reduce_fusion.1
  143.5 0.7 bitcast_divide_fusion
  (15 shorter events, 0.3 us)
Async XLA Ops:
  0.6 5.4 %copy-start = (f32[512,1024]{1,0:T(8,128)S(1)}, f32[512,1024]{1,0:T(8,128)}, u32[]{:S(2)}) copy-start(f32[512,1024]{1,0:T(8,128)} %param.2) | copy-start | bytes 6291460

commit v5 on v4

--- a/solution.py
+++ b/solution.py
@@ -1,6 +1,8 @@
 import jax
 import jax.numpy as jnp
 from jax import lax
+from jax.experimental import pallas as pl
+from jax.experimental.pallas import tpu as pltpu
 from jax.sharding import Mesh, PartitionSpec as P
 
 ITERS = 2
@@ -8,6 +10,7 @@
 SIZES = {"y": 4, "zh": 4, "x": 4, "zl": 4, "core": 2}
 PT = ("y", "zh", "x")
 CEN = ("zl", "core")
+WIDTH = 256
 
 
 def dot(a, b, dims):
@@ -18,6 +21,11 @@
         precision=lax.Precision.HIGH,
         preferred_element_type=jnp.float32,
     )
+
+
+def halves(x):
+    high = x.astype(jnp.bfloat16)
+    return high, (x - high.astype(jnp.float32)).astype(jnp.bfloat16)
 
 
 def group_size(axes):
@@ -45,19 +53,78 @@
 
 def lse(values, axis):
     top = jnp.max(values, axis=axis, keepdims=True)
-    expo = jnp.exp(values - top)
-    return jnp.squeeze(top, axis), expo, jnp.squeeze(top, axis) + jnp.log(jnp.sum(expo, axis=axis))
+    return top + jnp.log(jnp.sum(jnp.exp(values - top), axis=axis, keepdims=True))
+
+
+def first_kernel(split, points, centroids, logits, local, xs, cs, ordered, chigh, clow, xsem, csem):
+    ny, nz, nx, rows = split
+    chunk = nz * nx * rows
+    xcopies = [
+        pltpu.make_async_copy(points.at[pl.ds(i * WIDTH, WIDTH)], xs.at[pl.ds(i * WIDTH, WIDTH)], xsem.at[i])
+        for i in range(points.shape[0] // WIDTH)
+    ]
+    ccopies = [
+        pltpu.make_async_copy(centroids.at[pl.ds(i * chunk, chunk)], cs.at[pl.ds(i * chunk, chunk)], csem.at[i])
+        for i in range(ny)
+    ]
+    for copy in ccopies + xcopies:
+        copy.start()
+    for y in range(ny):
+        ccopies[y].wait()
+        for z in range(nz):
+            for x in range(nx):
+                here = y * chunk + (z * nx + x) * rows
+                there = y * chunk + (x * nz + z) * rows
+                ordered[there : there + rows, :] = cs[here : here + rows, :]
+        part = slice(y * chunk, (y + 1) * chunk)
+        chigh[part, :], clow[part, :] = halves(ordered[part, :])
+    nt = (((1,), (1,)), ((), ()))
+    for i, copy in enumerate(xcopies):
+        copy.wait()
+        part = slice(i * WIDTH, (i + 1) * WIDTH)
+        high, low = halves(xs[part, :])
+        value = lax.dot_general(chigh[...], high, nt, preferred_element_type=jnp.float32)
+        value += lax.dot_general(chigh[...], low, nt, preferred_element_type=jnp.float32)
+        value += lax.dot_general(clow[...], high, nt, preferred_element_type=jnp.float32)
+        value = value / TAU
+        logits[:, part] = value
+        local[:, part] = lse(value, 0)
+
+
+def first_logits(points, centroids, split):
+    n, d = points.shape
+    k = centroids.shape[0]
+    return pl.pallas_call(
+        lambda *refs: first_kernel(split, *refs),
+        out_shape=(
+            jax.ShapeDtypeStruct((k, n), jnp.float32),
+            jax.ShapeDtypeStruct((1, n), jnp.float32),
+        ),
+        in_specs=[pl.BlockSpec(memory_space=pltpu.HBM)] * 2,
+        out_specs=(pl.BlockSpec(memory_space=pltpu.VMEM),) * 2,
+        scratch_shapes=[
+            pltpu.VMEM((n, d), jnp.float32),
+            pltpu.VMEM((k, d), jnp.float32),
+            pltpu.VMEM((k, d), jnp.float32),
+            pltpu.VMEM((k, d), jnp.bfloat16),
+            pltpu.VMEM((k, d), jnp.bfloat16),
+            pltpu.SemaphoreType.DMA((n // WIDTH,)),
+            pltpu.SemaphoreType.DMA((split[0],)),
+        ],
+        compiler_params=pltpu.CompilerParams(vmem_limit_bytes=60 * 2**20),
+    )(points, centroids)
 
 
 def shards(points, centroids):
     split = tuple(lax.axis_size(axis) for axis in PT)
-    current = centroids.reshape(split + (-1, centroids.shape[1])).swapaxes(1, 2).reshape(centroids.shape)
+    split += (centroids.shape[0] // (split[0] * split[1] * split[2]),)
+    logits, local = first_logits(points, centroids, split)
     for turn in range(ITERS):
-        logits = dot(points, current, ((1,), (1,))) / TAU
-        top, expo, local = lse(logits, 1)
-        _, _, total = lse(gather(local, CEN), 0)
-        resp = expo * jnp.exp(top - total)[:, None]
-        weighted = dot(resp, points, ((0,), (0,)))
+        if turn:
+            logits = dot(current, points, ((1,), (1,))) / TAU
+            local = lse(logits, 0)
+        total = lse(gather(local, CEN), 0)[0, 0]
+        weighted = dot(jnp.exp(logits - total[None]), points, ((1,), (0,)))
         part = scatter_sum(weighted, ("y", "x"))
         if turn < ITERS - 1:
             mine = renormalise(jnp.sum(gather(part, ("zh",)), axis=0))

time: 145 us -> 143 us (0.986)
  Pallas kernels: 0 us -> 4.66 us
  local copies, waits for them, and re-layouts: 5.53 us -> 0.88 us
    reshape x3 -> x0, local copies, waits for them, and re-layouts: 5.33 us -> none  [shards(): centroids.reshape(split + (-1, centroids.shape[1])).swapaxes(1, 2)]
    pallas_call x0 -> x1, Pallas kernels: none -> 4.66 us  [first_logits(): pl.pallas_call(lambda *refs: first_kernel(split, *refs), out_shape=(jax.S...]
    dot_general x4 -> x3, matrix products: 5.51 us -> 4.29 us  [dot(): lax.dot_general(a, b, (dims, ((), ())), precision=lax.Precision.HIGH, pre...]
where the time goes in v5:
time: 143 us; the launch traced here: 142 us
  blocking collectives  130 us (91%)
  Pallas kernels  4.66 us (3%)
  matrix products  4.29 us (3%)
  other arithmetic  1.43 us (1%)
    all_to_all x4, blocking collectives, gather(): return lax.all_to_all(copies, axes, split_axis=0, concat_axis=0, tiled=True)  75.7 us
    all_to_all x3, blocking collectives, scatter_sum(): lax.all_to_all(blocks, axes, split_axis=0, concat_axis=0, tiled=True)  54.5 us
    pallas_call x1, Pallas kernels, first_logits(): pl.pallas_call(lambda *refs: first_kernel(split, *refs), out_shape=(jax.S...  4.66 us
    dot_general x3, matrix products, dot(): lax.dot_general(a, b, (dims, ((), ())), precision=lax.Precision.HIGH, pre...  4.29 us

profile of v5, /device:TPU:1, one launch (start us, length us, event | category | flops | bytes accessed | tf_op | source)
XLA Modules:
  0.0 142.2 jit_solution(1905345365812865160)
XLA Ops:
  0.6 0.0 copy-start
  0.6 4.7 %shard_map.41 = (f32[256,512]{1,0:T(8,128)}, f32[1,512]{1,0:T(1,128)}) custom-call(f32[512,1024]{1,0:T(8,128)} %refs_0_.1, f32[256,1024]{1,0:T(8,128)} %refs_1_.1), custom_call_target="tpu_custom_call" | custom-call | tf_op jit(solution)/shard_map/pallas_call | solution.py:97
  5.3 0.7 broadcast_in_dim.11
  6.0 14.2 %all_to_all.35 = f32[8,1,512]{2,1,0:T(1,128)S(1)} all-to-all(f32[8,1,512]{2,1,0:T(1,128)S(1)} %broadcast_in_dim.11), channel_id=1, replica_groups=mesh['y'=4,'zh'=4,'x'=4,'zl'=4,'core'=2] {'zl','core'}, dimensions={0} | all-to-all | bytes 32768 | tf_op jit(solution)/shard_map/all_to_all | solution.py:41
  20.2 0.0 copy-done
  20.2 2.1 %fusion.3 = f32[256,1024]{1,0:T(8,128)S(1)} fusion(f32[512,1024]{1,0:T(8,128)S(1)} %copy-done, f32[256,512]{1,0:T(8,128)} %get-tuple-element.4, f32[512]{0:T(512)S(1)} %log_add_fusion.2), kind=kOutput, calls=%fused_computation.5 | convolution fusion | flops 805437440 | bytes 3672064 | tf_op jit(solution)/shard_map/dot_general | solution.py:17
  22.4 20.7 %all_to_all.36 = f32[16,16,1024]{2,1,0:T(8,128)S(1)} all-to-all(f32[16,16,1024]{2,1,0:T(8,128)S(1)} %bitcast.11), channel_id=1, replica_groups=mesh['y'=4,'zh'=4,'x'=4,'zl'=4,'core'=2] {'y','x'}, dimensions={0} | all-to-all | bytes 2097152 | tf_op jit(solution)/shard_map/all_to_all | solution.py:47
  43.1 0.1 reduce_sum.84
  43.2 28.8 %all_to_all.37 = f32[4,16,1024]{2,1,0:T(8,128)S(1)} all-to-all(f32[4,16,1024]{2,1,0:T(8,128)S(1)} %broadcast_in_dim.12), channel_id=1, replica_groups=mesh['y'=4,'zh'=4,'x'=4,'zl'=4,'core'=2] {'zh'}, dimensions={0} | all-to-all | bytes 524288 | tf_op jit(solution)/shard_map/all_to_all | solution.py:41
  72.0 0.1 multiply_reduce_fusion
  72.2 0.1 broadcast_divide_fusion
  72.3 0.1 broadcast_in_dim.13
  72.4 16.0 %all_to_all.38 = f32[16,16,1024]{2,1,0:T(8,128)S(1)} all-to-all(f32[16,16,1024]{2,1,0:T(8,128)S(1)} %broadcast_in_dim.13), channel_id=1, replica_groups=mesh['y'=4,'zh'=4,'x'=4,'zl'=4,'core'=2] {'y','x'}, dimensions={0} | all-to-all | bytes 2097152 | tf_op jit(solution)/shard_map/all_to_all | solution.py:41
  88.4 1.1 fusion.12
  89.5 0.1 exponential_reduce_fusion
  89.6 16.7 %all_to_all.39 = f32[8,1,512]{2,1,0:T(1,128)S(1)} all-to-all(f32[8,1,512]{2,1,0:T(1,128)S(1)} %broadcast_in_dim.14), channel_id=1, replica_groups=mesh['y'=4,'zh'=4,'x'=4,'zl'=4,'core'=2] {'zl','core'}, dimensions={0} | all-to-all | bytes 32768 | tf_op jit(solution)/shard_map/all_to_all | solution.py:41
  106.4 0.0 copy-start.1
  106.4 1.1 fusion
  107.5 18.9 %all_to_all.40 = f32[16,16,1024]{2,1,0:T(8,128)S(1)} all-to-all(f32[16,16,1024]{2,1,0:T(8,128)S(1)} %bitcast.12), channel_id=1, replica_groups=mesh['y'=4,'zh'=4,'x'=4,'zl'=4,'core'=2] {'y','x'}, dimensions={0} | all-to-all | bytes 2097152 | tf_op jit(solution)/shard_map/all_to_all | solution.py:47
  126.3 0.0 copy-done.1
  126.4 0.1 reduce_sum.89
  126.4 14.9 %all_to_all.41 = f32[4,4,1024]{2,1,0:T(4,128)S(1)} all-to-all(f32[4,4,1024]{2,1,0:T(4,128)S(1)} %reshape.125), channel_id=1, replica_groups=mesh['y'=4,'zh'=4,'x'=4,'zl'=4,'core'=2] {'zh'}, dimensions={0} | all-to-all | bytes 131072 | tf_op jit(solution)/shard_map/all_to_all | solution.py:47
  141.4 0.1 multiply_reduce_fusion.1
  141.5 0.7 bitcast_divide_fusion
  (14 shorter events, 0.2 us)
Async XLA Ops:
  0.6 19.6 %copy-start = (f32[512,1024]{1,0:T(8,128)S(1)}, f32[512,1024]{1,0:T(8,128)}, u32[]{:S(2)}) copy-start(f32[512,1024]{1,0:T(8,128)} %refs_0_.1) | copy-start | bytes 6291460
  106.4 20.0 %copy-start.1 = (f32[512]{0:T(512)}, f32[512]{0:T(512)S(1)}, u32[]{:S(2)}) copy-start(f32[512]{0:T(512)S(1)} %log_add_fusion) | copy-start | bytes 6148

commit v6 on v5

--- a/solution.py
+++ b/solution.py
@@ -10,7 +10,6 @@
 SIZES = {"y": 4, "zh": 4, "x": 4, "zl": 4, "core": 2}
 PT = ("y", "zh", "x")
 CEN = ("zl", "core")
-WIDTH = 256
 
 
 def dot(a, b, dims):
@@ -56,39 +55,40 @@
     return top + jnp.log(jnp.sum(jnp.exp(values - top), axis=axis, keepdims=True))
 
 
-def first_kernel(split, points, centroids, logits, local, xs, cs, ordered, chigh, clow, xsem, csem):
+PIECES = 2
+
+
+def first_kernel(split, points, centroids, logits, local, xs, cs, ordered, xsem, csem):
     ny, nz, nx, rows = split
-    chunk = nz * nx * rows
-    xcopies = [
-        pltpu.make_async_copy(points.at[pl.ds(i * WIDTH, WIDTH)], xs.at[pl.ds(i * WIDTH, WIDTH)], xsem.at[i])
-        for i in range(points.shape[0] // WIDTH)
-    ]
-    ccopies = [
-        pltpu.make_async_copy(centroids.at[pl.ds(i * chunk, chunk)], cs.at[pl.ds(i * chunk, chunk)], csem.at[i])
-        for i in range(ny)
-    ]
-    for copy in ccopies + xcopies:
-        copy.start()
-    for y in range(ny):
-        ccopies[y].wait()
-        for z in range(nz):
-            for x in range(nx):
-                here = y * chunk + (z * nx + x) * rows
-                there = y * chunk + (x * nz + z) * rows
-                ordered[there : there + rows, :] = cs[here : here + rows, :]
-        part = slice(y * chunk, (y + 1) * chunk)
-        chigh[part, :], clow[part, :] = halves(ordered[part, :])
+    width = points.shape[1] // PIECES
+    columns = [slice(i * width, (i + 1) * width) for i in range(PIECES)]
+    ccopies = [pltpu.make_async_copy(centroids.at[:, c], cs.at[:, c], csem.at[i]) for i, c in enumerate(columns)]
+    xcopies = [pltpu.make_async_copy(points.at[:, c], xs.at[:, c], xsem.at[i]) for i, c in enumerate(columns)]
+    for ccopy, xcopy in zip(ccopies, xcopies):
+        ccopy.start()
+        xcopy.start()
     nt = (((1,), (1,)), ((), ()))
-    for i, copy in enumerate(xcopies):
-        copy.wait()
-        part = slice(i * WIDTH, (i + 1) * WIDTH)
-        high, low = halves(xs[part, :])
-        value = lax.dot_general(chigh[...], high, nt, preferred_element_type=jnp.float32)
-        value += lax.dot_general(chigh[...], low, nt, preferred_element_type=jnp.float32)
-        value += lax.dot_general(clow[...], high, nt, preferred_element_type=jnp.float32)
-        value = value / TAU
-        logits[:, part] = value
-        local[:, part] = lse(value, 0)
+    total = None
+    for i, c in enumerate(columns):
+        ccopies[i].wait()
+        for y in range(ny):
+            for z in range(nz):
+                for x in range(nx):
+                    here = ((y * nz + z) * nx + x) * rows
+                    there = ((y * nx + x) * nz + z) * rows
+                    ordered[there : there + rows, c] = cs[here : here + rows, c]
+        chigh, clow = halves(ordered[:, c])
+        xcopies[i].wait()
+        high, low = halves(xs[:, c])
+        value = lax.dot_general(chigh, high, nt, preferred_element_type=jnp.float32)
+        value += lax.dot_general(chigh, low, nt, preferred_element_type=jnp.float32)
+        value += lax.dot_general(clow, high, nt, preferred_element_type=jnp.float32)
+        if i:
+            value += logits[...]
+        if i == PIECES - 1:
+            value = value / TAU
+            local[...] = lse(value, 0)
+        logits[...] = value
 
 
 def first_logits(points, centroids, split):
@@ -106,12 +106,10 @@
             pltpu.VMEM((n, d), jnp.float32),
             pltpu.VMEM((k, d), jnp.float32),
             pltpu.VMEM((k, d), jnp.float32),
-            pltpu.VMEM((k, d), jnp.bfloat16),
-            pltpu.VMEM((k, d), jnp.bfloat16),
-            pltpu.SemaphoreType.DMA((n // WIDTH,)),
-            pltpu.SemaphoreType.DMA((split[0],)),
+            pltpu.SemaphoreType.DMA((PIECES,)),
+            pltpu.SemaphoreType.DMA((PIECES,)),
         ],
-        compiler_params=pltpu.CompilerParams(vmem_limit_bytes=60 * 2**20),
+        compiler_params=pltpu.CompilerParams(vmem_limit_bytes=52 * 2**20 + 640 * 2**10),
     )(points, centroids)
 
 

time: 143 us -> 139 us (0.972)
  Pallas kernels: 4.66 us -> 2.99 us
    pallas_call x1, Pallas kernels: 4.66 us -> 2.99 us  [first_logits(): pl.pallas_call(lambda *refs: first_kernel(split, *refs), out_shape=(jax.S...]
where the time goes in v6:
time: 139 us
  blocking collectives  130 us (94%)
  matrix products  3.25 us (2%)
  Pallas kernels  2.99 us (2%)
  other arithmetic  1.43 us (1%)
    all_to_all x4, blocking collectives, gather(): return lax.all_to_all(copies, axes, split_axis=0, concat_axis=0, tiled=True)  75.7 us
    all_to_all x3, blocking collectives, scatter_sum(): lax.all_to_all(blocks, axes, split_axis=0, concat_axis=0, tiled=True)  54.5 us
    dot_general x3, matrix products, dot(): lax.dot_general(a, b, (dims, ((), ())), precision=lax.Precision.HIGH, pre...  3.25 us
    pallas_call x1, Pallas kernels, first_logits(): pl.pallas_call(lambda *refs: first_kernel(split, *refs), out_shape=(jax.S...  2.99 us

profile of v6, /device:TPU:1, one launch (start us, length us, event | category | flops | bytes accessed | tf_op | source)
XLA Modules:
  0.0 138.9 jit_solution(13814502052049476267)
XLA Ops:
  0.6 0.0 copy-start
  0.6 3.0 %shard_map.41 = (f32[256,512]{1,0:T(8,128)S(1)}, f32[1,512]{1,0:T(1,128)S(1)}) custom-call(f32[512,1024]{1,0:T(8,128)} %refs_0_.1, f32[256,1024]{1,0:T(8,128)} %refs_1_.1), custom_call_target="tpu_custom_call" | custom-call | tf_op jit(solution)/shard_map/pallas_call | solution.py:97
  3.7 14.2 %all_to_all.35 = f32[8,1,512]{2,1,0:T(1,128)S(1)} all-to-all(f32[8,1,512]{2,1,0:T(1,128)S(1)} %broadcast_in_dim.11), channel_id=1, replica_groups=mesh['y'=4,'zh'=4,'x'=4,'zl'=4,'core'=2] {'zl','core'}, dimensions={0} | all-to-all | bytes 32768 | tf_op jit(solution)/shard_map/all_to_all | solution.py:40
  17.9 0.0 copy-done
  17.9 1.1 fusion.3
  19.0 20.7 %all_to_all.36 = f32[16,16,1024]{2,1,0:T(8,128)S(1)} all-to-all(f32[16,16,1024]{2,1,0:T(8,128)S(1)} %bitcast.12), channel_id=1, replica_groups=mesh['y'=4,'zh'=4,'x'=4,'zl'=4,'core'=2] {'y','x'}, dimensions={0} | all-to-all | bytes 2097152 | tf_op jit(solution)/shard_map/all_to_all | solution.py:46
  39.7 0.1 reduce_sum.84
  39.8 28.8 %all_to_all.37 = f32[4,16,1024]{2,1,0:T(8,128)S(1)} all-to-all(f32[4,16,1024]{2,1,0:T(8,128)S(1)} %broadcast_in_dim.12), channel_id=1, replica_groups=mesh['y'=4,'zh'=4,'x'=4,'zl'=4,'core'=2] {'zh'}, dimensions={0} | all-to-all | bytes 524288 | tf_op jit(solution)/shard_map/all_to_all | solution.py:40
  68.7 0.1 multiply_reduce_fusion
  68.8 0.1 broadcast_divide_fusion
  68.9 0.1 broadcast_in_dim.13
  69.0 16.0 %all_to_all.38 = f32[16,16,1024]{2,1,0:T(8,128)S(1)} all-to-all(f32[16,16,1024]{2,1,0:T(8,128)S(1)} %broadcast_in_dim.13), channel_id=1, replica_groups=mesh['y'=4,'zh'=4,'x'=4,'zl'=4,'core'=2] {'y','x'}, dimensions={0} | all-to-all | bytes 2097152 | tf_op jit(solution)/shard_map/all_to_all | solution.py:40
  85.0 1.1 fusion.12
  86.1 0.1 exponential_reduce_fusion
  86.3 16.7 %all_to_all.39 = f32[8,1,512]{2,1,0:T(1,128)S(1)} all-to-all(f32[8,1,512]{2,1,0:T(1,128)S(1)} %broadcast_in_dim.14), channel_id=1, replica_groups=mesh['y'=4,'zh'=4,'x'=4,'zl'=4,'core'=2] {'zl','core'}, dimensions={0} | all-to-all | bytes 32768 | tf_op jit(solution)/shard_map/all_to_all | solution.py:40
  103.0 0.0 copy-start.1
  103.0 1.1 fusion
  104.1 18.9 %all_to_all.40 = f32[16,16,1024]{2,1,0:T(8,128)S(1)} all-to-all(f32[16,16,1024]{2,1,0:T(8,128)S(1)} %bitcast.13), channel_id=1, replica_groups=mesh['y'=4,'zh'=4,'x'=4,'zl'=4,'core'=2] {'y','x'}, dimensions={0} | all-to-all | bytes 2097152 | tf_op jit(solution)/shard_map/all_to_all | solution.py:46
  123.0 0.0 copy-done.1
  123.0 0.1 reduce_sum.89
  123.1 14.9 %all_to_all.41 = f32[4,4,1024]{2,1,0:T(4,128)S(1)} all-to-all(f32[4,4,1024]{2,1,0:T(4,128)S(1)} %reshape.125), channel_id=1, replica_groups=mesh['y'=4,'zh'=4,'x'=4,'zl'=4,'core'=2] {'zh'}, dimensions={0} | all-to-all | bytes 131072 | tf_op jit(solution)/shard_map/all_to_all | solution.py:46
  138.0 0.1 multiply_reduce_fusion.1
  138.2 0.7 bitcast_divide_fusion
  (15 shorter events, 0.3 us)
Async XLA Ops:
  0.6 17.3 %copy-start = (f32[512,1024]{1,0:T(8,128)S(1)}, f32[512,1024]{1,0:T(8,128)}, u32[]{:S(2)}) copy-start(f32[512,1024]{1,0:T(8,128)} %refs_0_.1) | copy-start | bytes 6291460
  103.0 20.0 %copy-start.1 = (f32[512]{0:T(512)}, f32[512]{0:T(512)S(1)}, u32[]{:S(2)}) copy-start(f32[512]{0:T(512)S(1)} %log_add_fusion) | copy-start | bytes 6148

commit v7 on v6

--- a/solution.py
+++ b/solution.py
@@ -44,6 +44,12 @@
     n = group_size(axes)
     blocks = rows.reshape(n, rows.shape[0] // n, rows.shape[1])
     return jnp.sum(lax.all_to_all(blocks, axes, split_axis=0, concat_axis=0, tiled=True), axis=0)
+
+
+def ring_sum(part):
+    for pairs in (((0, 1), (2, 3)), ((1, 2), (3, 0))):
+        part += lax.ppermute(part, "zh", [p for a, b in pairs for p in ((a, b), (b, a))])
+    return part
 
 
 def renormalise(weighted):
@@ -125,7 +131,7 @@
         weighted = dot(jnp.exp(logits - total[None]), points, ((1,), (0,)))
         part = scatter_sum(weighted, ("y", "x"))
         if turn < ITERS - 1:
-            mine = renormalise(jnp.sum(gather(part, ("zh",)), axis=0))
+            mine = renormalise(ring_sum(part))
             current = gather(mine, ("y", "x")).reshape(centroids.shape)
     owned = renormalise(scatter_sum(part, ("zh",)))
     return owned[None], total

time: 139 us -> 139 us (level); the launches traced: 139 us -> 137 us
  blocking collectives: 130 us -> 104 us
  starting transfers between devices: 0 us -> 13.9 us
  waiting for transfers between devices: 0 us -> 10.6 us
    all_to_all x4 -> x3, blocking collectives: 75.7 us -> 46 us  [gather(): return lax.all_to_all(copies, axes, split_axis=0, concat_axis=0, tiled=True)]
    ppermute x0 -> x2, starting transfers between devices: none -> 13.9 us  [ring_sum(): lax.ppermute(part, 'zh', [p for a, b in pairs for p in ((a, b), (b, a))])]
    ppermute x0 -> x2, waiting for transfers between devices: none -> 10.6 us  [ring_sum(): lax.ppermute(part, 'zh', [p for a, b in pairs for p in ((a, b), (b, a))])]
    all_to_all x3, blocking collectives: 54.5 us -> 58.2 us  [scatter_sum(): lax.all_to_all(blocks, axes, split_axis=0, concat_axis=0, tiled=True)]
  transfers between devices with their start and end apart: 0 -> 2, of which waited for: 0 -> 2; matrix products, arithmetic and copies ran while one was open for 0% -> 0% of each run, Pallas kernels for 0% -> 0%
where the time goes in v7:
time: 139 us; the launch traced here: 137 us
  blocking collectives  104 us (75%)
  starting transfers between devices  13.9 us (10%)
  waiting for transfers between devices  10.6 us (8%)
  matrix products  3.25 us (2%)
  Pallas kernels  2.99 us (2%)
  other arithmetic  1.42 us (1%)
    all_to_all x3, blocking collectives, scatter_sum(): lax.all_to_all(blocks, axes, split_axis=0, concat_axis=0, tiled=True)  58.2 us
    all_to_all x3, blocking collectives, gather(): return lax.all_to_all(copies, axes, split_axis=0, concat_axis=0, tiled=True)  46 us
    ppermute x2, starting transfers between devices, ring_sum(): lax.ppermute(part, 'zh', [p for a, b in pairs for p in ((a, b), (b, a))])  13.9 us
    ppermute x2, waiting for transfers between devices, ring_sum(): lax.ppermute(part, 'zh', [p for a, b in pairs for p in ((a, b), (b, a))])  10.6 us
    dot_general x3, matrix products, dot(): lax.dot_general(a, b, (dims, ((), ())), precision=lax.Precision.HIGH, pre...  3.25 us
    pallas_call x1, Pallas kernels, first_logits(): pl.pallas_call(lambda *refs: first_kernel(split, *refs), out_shape=(jax.S...  2.99 us
  transfers between devices with their start and end apart: 2, of which 2 were waited for; matrix products, arithmetic and copies ran while one was open for 0% of the time, Pallas kernels for 0%

profile of v7, /device:TPU:1, one launch (start us, length us, event | category | flops | bytes accessed | tf_op | source)
XLA Modules:
  0.0 137.4 jit_solution(10289546244088180360)
XLA Ops:
  0.6 0.0 copy-start
  0.6 3.0 %shard_map.41 = (f32[256,512]{1,0:T(8,128)S(1)}, f32[1,512]{1,0:T(1,128)S(1)}) custom-call(f32[512,1024]{1,0:T(8,128)} %refs_0_.1, f32[256,1024]{1,0:T(8,128)} %refs_1_.1), custom_call_target="tpu_custom_call" | custom-call | tf_op jit(solution)/shard_map/pallas_call | solution.py:103
  3.7 14.2 %all_to_all.30 = f32[8,1,512]{2,1,0:T(1,128)S(1)} all-to-all(f32[8,1,512]{2,1,0:T(1,128)S(1)} %broadcast_in_dim.9), channel_id=1, replica_groups=mesh['y'=4,'zh'=4,'x'=4,'zl'=4,'core'=2] {'zl','core'}, dimensions={0} | all-to-all | bytes 32768 | tf_op jit(solution)/shard_map/all_to_all | solution.py:40
  17.9 0.0 copy-done
  17.9 1.1 fusion.3
  19.0 20.7 %all_to_all.31 = f32[16,16,1024]{2,1,0:T(8,128)S(1)} all-to-all(f32[16,16,1024]{2,1,0:T(8,128)S(1)} %bitcast.12), channel_id=1, replica_groups=mesh['y'=4,'zh'=4,'x'=4,'zl'=4,'core'=2] {'y','x'}, dimensions={0} | all-to-all | bytes 2097152 | tf_op jit(solution)/shard_map/all_to_all | solution.py:46
  39.7 0.1 reduce_sum.75
  39.8 8.8 %collective-permute-start = (f32[16,1024]{1,0:T(8,128)S(1)}, f32[16,1024]{1,0:T(8,128)S(1)}, u32[]{:S(2)}, u32[]{:S(2)}) collective-permute-start(f32[16,1024]{1,0:T(8,128)S(1)} %reduce_sum.75), channel_id=1, source_target_pairs={{0,32},{32,0},{64,96},{96,64},{1,33},{33,1},{65,97},{97,65},{2,34}... | collective-permute-start | bytes 196616 | tf_op jit(solution)/shard_map/ppermute | solution.py:51
  48.6 6.7 %collective-permute-done = f32[16,1024]{1,0:T(8,128)S(1)} collective-permute-done((f32[16,1024]{1,0:T(8,128)S(1)}, f32[16,1024]{1,0:T(8,128)S(1)}, u32[]{:S(2)}, u32[]{:S(2)}) %collective-permute-start) | collective-permute-done | bytes 65568 | tf_op jit(solution)/shard_map/ppermute | solution.py:51
  55.3 5.1 %collective-permute-start.1 = (f32[16,1024]{1,0:T(8,128)S(1)}, f32[16,1024]{1,0:T(8,128)S(1)}, u32[]{:S(2)}, u32[]{:S(2)}) collective-permute-start(f32[16,1024]{1,0:T(8,128)S(1)} %add.51), channel_id=1, source_target_pairs={{32,64},{64,32},{96,0},{0,96},{33,65},{65,33},{97,1},{1,97},{34,66... | collective-permute-start | bytes 196616 | tf_op jit(solution)/shard_map/ppermute | solution.py:51
  60.4 3.9 %collective-permute-done.1 = f32[16,1024]{1,0:T(8,128)S(1)} collective-permute-done((f32[16,1024]{1,0:T(8,128)S(1)}, f32[16,1024]{1,0:T(8,128)S(1)}, u32[]{:S(2)}, u32[]{:S(2)}) %collective-permute-start.1) | collective-permute-done | bytes 65568 | tf_op jit(solution)/shard_map/ppermute | solution.py:51
  64.4 0.1 multiply_reduce_fusion
  64.5 0.1 broadcast_divide_fusion
  64.6 0.1 broadcast_in_dim.10
  64.7 18.6 %all_to_all.32 = f32[16,16,1024]{2,1,0:T(8,128)S(1)} all-to-all(f32[16,16,1024]{2,1,0:T(8,128)S(1)} %broadcast_in_dim.10), channel_id=1, replica_groups=mesh['y'=4,'zh'=4,'x'=4,'zl'=4,'core'=2] {'y','x'}, dimensions={0} | all-to-all | bytes 2097152 | tf_op jit(solution)/shard_map/all_to_all | solution.py:40
  83.3 1.1 fusion.12
  84.4 0.1 exponential_reduce_fusion
  84.5 13.2 %all_to_all.33 = f32[8,1,512]{2,1,0:T(1,128)S(1)} all-to-all(f32[8,1,512]{2,1,0:T(1,128)S(1)} %broadcast_in_dim.11), channel_id=1, replica_groups=mesh['y'=4,'zh'=4,'x'=4,'zl'=4,'core'=2] {'zl','core'}, dimensions={0} | all-to-all | bytes 32768 | tf_op jit(solution)/shard_map/all_to_all | solution.py:40
  97.8 0.0 copy-start.1
  97.8 1.1 fusion
  98.9 18.9 %all_to_all.34 = f32[16,16,1024]{2,1,0:T(8,128)S(1)} all-to-all(f32[16,16,1024]{2,1,0:T(8,128)S(1)} %bitcast.13), channel_id=1, replica_groups=mesh['y'=4,'zh'=4,'x'=4,'zl'=4,'core'=2] {'y','x'}, dimensions={0} | all-to-all | bytes 2097152 | tf_op jit(solution)/shard_map/all_to_all | solution.py:46
  117.8 0.0 copy-done.1
  117.8 0.1 reduce_sum.79
  117.9 18.6 %all_to_all.35 = f32[4,4,1024]{2,1,0:T(4,128)S(1)} all-to-all(f32[4,4,1024]{2,1,0:T(4,128)S(1)} %reshape.110), channel_id=1, replica_groups=mesh['y'=4,'zh'=4,'x'=4,'zl'=4,'core'=2] {'zh'}, dimensions={0} | all-to-all | bytes 131072 | tf_op jit(solution)/shard_map/all_to_all | solution.py:46
  136.5 0.1 multiply_reduce_fusion.1
  136.7 0.7 bitcast_divide_fusion
  (14 shorter events, 0.2 us)
Async XLA Ops:
  0.6 17.3 %copy-start = (f32[512,1024]{1,0:T(8,128)S(1)}, f32[512,1024]{1,0:T(8,128)}, u32[]{:S(2)}) copy-start(f32[512,1024]{1,0:T(8,128)} %refs_0_.1) | copy-start | bytes 6291460
  39.8 15.6 %collective-permute-start = (f32[16,1024]{1,0:T(8,128)S(1)}, f32[16,1024]{1,0:T(8,128)S(1)}, u32[]{:S(2)}, u32[]{:S(2)}) collective-permute-start(f32[16,1024]{1,0:T(8,128)S(1)} %reduce_sum.75), channel_id=1, source_target_pairs={{0,32},{32,0},{64,96},{96,64},{1,33},{33,1},{65,97},{97,65},{2,34}... | collective-permute-start | bytes 196616 | tf_op jit(solution)/shard_map/ppermute | solution.py:51
  55.3 9.0 %collective-permute-start.1 = (f32[16,1024]{1,0:T(8,128)S(1)}, f32[16,1024]{1,0:T(8,128)S(1)}, u32[]{:S(2)}, u32[]{:S(2)}) collective-permute-start(f32[16,1024]{1,0:T(8,128)S(1)} %add.51), channel_id=1, source_target_pairs={{32,64},{64,32},{96,0},{0,96},{33,65},{65,33},{97,1},{1,97},{34,66... | collective-permute-start | bytes 196616 | tf_op jit(solution)/shard_map/ppermute | solution.py:51
  97.8 20.0 %copy-start.1 = (f32[512]{0:T(512)}, f32[512]{0:T(512)S(1)}, u32[]{:S(2)}) copy-start(f32[512]{0:T(512)S(1)} %log_add_fusion) | copy-start | bytes 6148

commit v8 on v6

--- a/solution.py
+++ b/solution.py
@@ -125,7 +125,7 @@
         weighted = dot(jnp.exp(logits - total[None]), points, ((1,), (0,)))
         part = scatter_sum(weighted, ("y", "x"))
         if turn < ITERS - 1:
-            mine = renormalise(jnp.sum(gather(part, ("zh",)), axis=0))
+            mine = renormalise(jnp.sum(lax.all_gather(part, "zh"), axis=0))
             current = gather(mine, ("y", "x")).reshape(centroids.shape)
     owned = renormalise(scatter_sum(part, ("zh",)))
     return owned[None], total

time: 139 us -> 133 us (0.957)
  blocking collectives: 130 us -> 123 us
    all_to_all x4 -> x3, blocking collectives: 75.7 us -> 43.2 us  [gather(): return lax.all_to_all(copies, axes, split_axis=0, concat_axis=0, tiled=True)]
    all_gather x0 -> x1, blocking collectives: none -> 22.4 us  [shards(): mine = renormalise(jnp.sum(lax.all_gather(part, 'zh'), axis=0))]
    all_to_all x3, blocking collectives: 54.5 us -> 57.4 us  [scatter_sum(): lax.all_to_all(blocks, axes, split_axis=0, concat_axis=0, tiled=True)]
where the time goes in v8:
time: 133 us; the launch traced here: 132 us
  blocking collectives  123 us (92%)
  matrix products  3.25 us (2%)
  Pallas kernels  2.99 us (2%)
  other arithmetic  1.43 us (1%)
    all_to_all x3, blocking collectives, scatter_sum(): lax.all_to_all(blocks, axes, split_axis=0, concat_axis=0, tiled=True)  57.4 us
    all_to_all x3, blocking collectives, gather(): return lax.all_to_all(copies, axes, split_axis=0, concat_axis=0, tiled=True)  43.2 us
    all_gather x1, blocking collectives, shards(): mine = renormalise(jnp.sum(lax.all_gather(part, 'zh'), axis=0))  22.4 us
    dot_general x3, matrix products, dot(): lax.dot_general(a, b, (dims, ((), ())), precision=lax.Precision.HIGH, pre...  3.25 us
    pallas_call x1, Pallas kernels, first_logits(): pl.pallas_call(lambda *refs: first_kernel(split, *refs), out_shape=(jax.S...  2.99 us

profile of v8, /device:TPU:1, one launch (start us, length us, event | category | flops | bytes accessed | tf_op | source)
XLA Modules:
  0.0 131.7 jit_solution(13470208544490778758)
XLA Ops:
  0.6 0.0 copy-start
  0.6 3.0 %shard_map.41 = (f32[256,512]{1,0:T(8,128)S(1)}, f32[1,512]{1,0:T(1,128)S(1)}) custom-call(f32[512,1024]{1,0:T(8,128)} %refs_0_.1, f32[256,1024]{1,0:T(8,128)} %refs_1_.1), custom_call_target="tpu_custom_call" | custom-call | tf_op jit(solution)/shard_map/pallas_call | solution.py:97
  3.7 14.2 %all_to_all.30 = f32[8,1,512]{2,1,0:T(1,128)S(1)} all-to-all(f32[8,1,512]{2,1,0:T(1,128)S(1)} %broadcast_in_dim.9), channel_id=1, replica_groups=mesh['y'=4,'zh'=4,'x'=4,'zl'=4,'core'=2] {'zl','core'}, dimensions={0} | all-to-all | bytes 32768 | tf_op jit(solution)/shard_map/all_to_all | solution.py:40
  17.9 0.0 copy-done
  17.9 1.1 fusion.3
  19.0 20.7 %all_to_all.31 = f32[16,16,1024]{2,1,0:T(8,128)S(1)} all-to-all(f32[16,16,1024]{2,1,0:T(8,128)S(1)} %bitcast.13), channel_id=1, replica_groups=mesh['y'=4,'zh'=4,'x'=4,'zl'=4,'core'=2] {'y','x'}, dimensions={0} | all-to-all | bytes 2097152 | tf_op jit(solution)/shard_map/all_to_all | solution.py:46
  39.7 0.1 reduce_sum.84
  39.8 22.4 %all-gather = f32[64,1024]{1,0:T(8,128)S(1)} all-gather(f32[16,1024]{1,0:T(8,128)S(1)} %reduce_sum.84), channel_id=2, replica_groups=mesh['y'=4,'zh'=4,'x'=4,'zl'=4,'core'=2] {'zh'}, dimensions={0}, use_global_device_ids=true | all-gather | bytes 327680 | tf_op jit(solution)/shard_map/all_gather | solution.py:128
  62.2 0.1 multiply_reduce_fusion
  62.4 0.1 broadcast_divide_fusion
  62.4 0.1 broadcast_in_dim.10
  62.6 14.6 %all_to_all.32 = f32[16,16,1024]{2,1,0:T(8,128)S(1)} all-to-all(f32[16,16,1024]{2,1,0:T(8,128)S(1)} %broadcast_in_dim.10), channel_id=1, replica_groups=mesh['y'=4,'zh'=4,'x'=4,'zl'=4,'core'=2] {'y','x'}, dimensions={0} | all-to-all | bytes 2097152 | tf_op jit(solution)/shard_map/all_to_all | solution.py:40
  77.2 1.1 fusion.12
  78.3 0.1 exponential_reduce_fusion
  78.4 14.5 %all_to_all.33 = f32[8,1,512]{2,1,0:T(1,128)S(1)} all-to-all(f32[8,1,512]{2,1,0:T(1,128)S(1)} %broadcast_in_dim.11), channel_id=1, replica_groups=mesh['y'=4,'zh'=4,'x'=4,'zl'=4,'core'=2] {'zl','core'}, dimensions={0} | all-to-all | bytes 32768 | tf_op jit(solution)/shard_map/all_to_all | solution.py:40
  92.9 0.0 copy-start.1
  93.0 1.1 fusion
  94.0 18.8 %all_to_all.34 = f32[16,16,1024]{2,1,0:T(8,128)S(1)} all-to-all(f32[16,16,1024]{2,1,0:T(8,128)S(1)} %bitcast.14), channel_id=1, replica_groups=mesh['y'=4,'zh'=4,'x'=4,'zl'=4,'core'=2] {'y','x'}, dimensions={0} | all-to-all | bytes 2097152 | tf_op jit(solution)/shard_map/all_to_all | solution.py:46
  112.9 0.0 copy-done.1
  112.9 0.1 reduce_sum.89
  113.0 17.9 %all_to_all.35 = f32[4,4,1024]{2,1,0:T(4,128)S(1)} all-to-all(f32[4,4,1024]{2,1,0:T(4,128)S(1)} %reshape.124), channel_id=1, replica_groups=mesh['y'=4,'zh'=4,'x'=4,'zl'=4,'core'=2] {'zh'}, dimensions={0} | all-to-all | bytes 131072 | tf_op jit(solution)/shard_map/all_to_all | solution.py:46
  130.9 0.1 multiply_reduce_fusion.1
  131.0 0.7 bitcast_divide_fusion
  (14 shorter events, 0.2 us)
Async XLA Ops:
  0.6 17.3 %copy-start = (f32[512,1024]{1,0:T(8,128)S(1)}, f32[512,1024]{1,0:T(8,128)}, u32[]{:S(2)}) copy-start(f32[512,1024]{1,0:T(8,128)} %refs_0_.1) | copy-start | bytes 6291460
  92.9 19.9 %copy-start.1 = (f32[512]{0:T(512)}, f32[512]{0:T(512)S(1)}, u32[]{:S(2)}) copy-start(f32[512]{0:T(512)S(1)} %log_add_fusion) | copy-start | bytes 6148

commit v9 on v8

--- a/solution.py
+++ b/solution.py
@@ -1,3 +1,5 @@
+import itertools
+
 import jax
 import jax.numpy as jnp
 from jax import lax
@@ -10,6 +12,7 @@
 SIZES = {"y": 4, "zh": 4, "x": 4, "zl": 4, "core": 2}
 PT = ("y", "zh", "x")
 CEN = ("zl", "core")
+PLANE = ("y", "x", "core")
 
 
 def dot(a, b, dims):
@@ -34,16 +37,29 @@
     return n
 
 
+def plane_groups():
+    ny, nx, nc = (lax.axis_size(axis) for axis in PLANE)
+    first = [(y * nx + x) * nc for y in range(ny) for x in range(nx)]
+    second = [(y * nx + x) * nc + 1 for x in range(nx) for y in range(ny)]
+    return [first, second]
+
+
+def swap(blocks, axes):
+    groups = plane_groups() if axes == PLANE else None
+    return lax.all_to_all(blocks, axes, split_axis=0, concat_axis=0, tiled=True, axis_index_groups=groups)
+
+
+def count(axes):
+    return group_size(axes[:2] if axes == PLANE else axes)
+
+
 def gather(block, axes):
-    n = group_size(axes)
-    copies = jnp.broadcast_to(block[None], (n,) + block.shape)
-    return lax.all_to_all(copies, axes, split_axis=0, concat_axis=0, tiled=True)
+    return swap(jnp.broadcast_to(block[None], (count(axes),) + block.shape), axes)
 
 
 def scatter_sum(rows, axes):
-    n = group_size(axes)
-    blocks = rows.reshape(n, rows.shape[0] // n, rows.shape[1])
-    return jnp.sum(lax.all_to_all(blocks, axes, split_axis=0, concat_axis=0, tiled=True), axis=0)
+    n = count(axes)
+    return jnp.sum(swap(rows.reshape(n, rows.shape[0] // n, rows.shape[1]), axes), axis=0)
 
 
 def renormalise(weighted):
@@ -60,6 +76,7 @@
 
 def first_kernel(split, points, centroids, logits, local, xs, cs, ordered, xsem, csem):
     ny, nz, nx, rows = split
+    core = lax.axis_index("core")
     width = points.shape[1] // PIECES
     columns = [slice(i * width, (i + 1) * width) for i in range(PIECES)]
     ccopies = [pltpu.make_async_copy(centroids.at[:, c], cs.at[:, c], csem.at[i]) for i, c in enumerate(columns)]
@@ -71,12 +88,16 @@
     total = None
     for i, c in enumerate(columns):
         ccopies[i].wait()
-        for y in range(ny):
-            for z in range(nz):
-                for x in range(nx):
+        for number in range(2):
+
+            @pl.when(core == number)
+            def _():
+                for y, z, x in itertools.product(range(ny), range(nz), range(nx)):
                     here = ((y * nz + z) * nx + x) * rows
-                    there = ((y * nx + x) * nz + z) * rows
+                    block = x * ny + y if number else y * nx + x
+                    there = (block * nz + z) * rows
                     ordered[there : there + rows, c] = cs[here : here + rows, c]
+
         chigh, clow = halves(ordered[:, c])
         xcopies[i].wait()
         high, low = halves(xs[:, c])
@@ -123,10 +144,10 @@
             local = lse(logits, 0)
         total = lse(gather(local, CEN), 0)[0, 0]
         weighted = dot(jnp.exp(logits - total[None]), points, ((1,), (0,)))
-        part = scatter_sum(weighted, ("y", "x"))
+        part = scatter_sum(weighted, PLANE)
         if turn < ITERS - 1:
             mine = renormalise(jnp.sum(lax.all_gather(part, "zh"), axis=0))
-            current = gather(mine, ("y", "x")).reshape(centroids.shape)
+            current = gather(mine, PLANE).reshape(centroids.shape)
     owned = renormalise(scatter_sum(part, ("zh",)))
     return owned[None], total
 

time: 133 us -> 133 us (level)
    all_to_all x6, blocking collectives: 101 us -> 102 us  [swap(): lax.all_to_all(blocks, axes, split_axis=0, concat_axis=0, tiled=True, axi...]
where the time goes in v9:
time: 133 us
  blocking collectives  124 us (93%)
  matrix products  3.25 us (2%)
  Pallas kernels  3 us (2%)
  other arithmetic  1.43 us (1%)
    all_to_all x6, blocking collectives, swap(): lax.all_to_all(blocks, axes, split_axis=0, concat_axis=0, tiled=True, axi...  102 us
    all_gather x1, blocking collectives, shards(): mine = renormalise(jnp.sum(lax.all_gather(part, 'zh'), axis=0))  22.2 us
    dot_general x3, matrix products, dot(): lax.dot_general(a, b, (dims, ((), ())), precision=lax.Precision.HIGH, pre...  3.25 us
    pallas_call x1, Pallas kernels, first_logits(): pl.pallas_call(lambda *refs: first_kernel(split, *refs), out_shape=(jax.S...  3 us

profile of v9, /device:TPU:1, one launch (start us, length us, event | category | flops | bytes accessed | tf_op | source)
XLA Modules:
  0.0 132.8 jit_solution(6545160775674328101)
XLA Ops:
  0.6 0.0 copy-start
  0.6 3.0 %shard_map.41 = (f32[256,512]{1,0:T(8,128)S(1)}, f32[1,512]{1,0:T(1,128)S(1)}) custom-call(f32[512,1024]{1,0:T(8,128)} %refs_0_.1, f32[256,1024]{1,0:T(8,128)} %refs_1_.1), custom_call_target="tpu_custom_call" | custom-call | tf_op jit(solution)/shard_map/pallas_call | solution.py:118
  3.7 14.2 %all_to_all.30 = f32[8,1,512]{2,1,0:T(1,128)S(1)} all-to-all(f32[8,1,512]{2,1,0:T(1,128)S(1)} %broadcast_in_dim.9), channel_id=1, replica_groups=mesh['y'=4,'zh'=4,'x'=4,'zl'=4,'core'=2] {'zl','core'}, dimensions={0} | all-to-all | bytes 32768 | tf_op jit(solution)/shard_map/all_to_all | solution.py:49
  17.9 0.0 copy-done
  17.9 1.1 fusion.3
  19.0 21.0 %all_to_all.31 = f32[16,16,1024]{2,1,0:T(8,128)S(1)} all-to-all(f32[16,16,1024]{2,1,0:T(8,128)S(1)} %bitcast.13), channel_id=1, replica_groups={{0,8,16,24,128,136,144,152,256,264,272,280,384,392,400,408},{1,129,257,..., dimensions={0} | all-to-all | bytes 2097152 | tf_op jit(solution)/shard_map/all_to_all | solution.py:49
  40.0 0.1 reduce_sum.84
  40.1 22.2 %all-gather = f32[64,1024]{1,0:T(8,128)S(1)} all-gather(f32[16,1024]{1,0:T(8,128)S(1)} %reduce_sum.84), channel_id=2, replica_groups=mesh['y'=4,'zh'=4,'x'=4,'zl'=4,'core'=2] {'zh'}, dimensions={0}, use_global_device_ids=true | all-gather | bytes 327680 | tf_op jit(solution)/shard_map/all_gather | solution.py:149
  62.2 0.1 multiply_reduce_fusion
  62.4 0.1 broadcast_divide_fusion
  62.5 0.1 broadcast_in_dim.10
  62.6 14.9 %all_to_all.32 = f32[16,16,1024]{2,1,0:T(8,128)S(1)} all-to-all(f32[16,16,1024]{2,1,0:T(8,128)S(1)} %broadcast_in_dim.10), channel_id=1, replica_groups={{0,8,16,24,128,136,144,152,256,264,272,280,384,392,400,408},{1,129,257,..., dimensions={0} | all-to-all | bytes 2097152 | tf_op jit(solution)/shard_map/all_to_all | solution.py:49
  77.5 1.1 fusion.12
  78.6 0.1 exponential_reduce_fusion
  78.8 14.1 %all_to_all.33 = f32[8,1,512]{2,1,0:T(1,128)S(1)} all-to-all(f32[8,1,512]{2,1,0:T(1,128)S(1)} %broadcast_in_dim.11), channel_id=1, replica_groups=mesh['y'=4,'zh'=4,'x'=4,'zl'=4,'core'=2] {'zl','core'}, dimensions={0} | all-to-all | bytes 32768 | tf_op jit(solution)/shard_map/all_to_all | solution.py:49
  93.0 0.0 copy-start.1
  93.0 1.1 fusion
  94.1 19.1 %all_to_all.34 = f32[16,16,1024]{2,1,0:T(8,128)S(1)} all-to-all(f32[16,16,1024]{2,1,0:T(8,128)S(1)} %bitcast.14), channel_id=1, replica_groups={{0,8,16,24,128,136,144,152,256,264,272,280,384,392,400,408},{1,129,257,..., dimensions={0} | all-to-all | bytes 2097152 | tf_op jit(solution)/shard_map/all_to_all | solution.py:49
  113.2 0.0 copy-done.1
  113.2 0.1 reduce_sum.89
  113.3 18.6 %all_to_all.35 = f32[4,4,1024]{2,1,0:T(4,128)S(1)} all-to-all(f32[4,4,1024]{2,1,0:T(4,128)S(1)} %reshape.124), channel_id=1, replica_groups=mesh['y'=4,'zh'=4,'x'=4,'zl'=4,'core'=2] {'zh'}, dimensions={0} | all-to-all | bytes 131072 | tf_op jit(solution)/shard_map/all_to_all | solution.py:49
  131.9 0.1 multiply_reduce_fusion.1
  132.1 0.7 bitcast_divide_fusion
  (14 shorter events, 0.2 us)
Async XLA Ops:
  0.6 17.3 %copy-start = (f32[512,1024]{1,0:T(8,128)S(1)}, f32[512,1024]{1,0:T(8,128)}, u32[]{:S(2)}) copy-start(f32[512,1024]{1,0:T(8,128)} %refs_0_.1) | copy-start | bytes 6291460
  93.0 20.2 %copy-start.1 = (f32[512]{0:T(512)}, f32[512]{0:T(512)S(1)}, u32[]{:S(2)}) copy-start(f32[512]{0:T(512)S(1)} %log_add_fusion) | copy-start | bytes 6148

commit v10 on v8

--- a/solution.py
+++ b/solution.py
@@ -46,6 +46,19 @@
     return jnp.sum(lax.all_to_all(blocks, axes, split_axis=0, concat_axis=0, tiled=True), axis=0)
 
 
+def exchange(keep, send, pairs):
+    return keep + lax.ppermute(send, "zh", [p for a, b in pairs for p in ((a, b), (b, a))])
+
+
+def ring_scatter(rows):
+    z = lax.axis_index("zh")
+    for upper, pairs in (((0, 3), ((0, 1), (2, 3))), ((0, 1), ((1, 2), (3, 0)))):
+        top, low = jnp.split(rows, 2)
+        up = (z == upper[0]) | (z == upper[1])
+        rows = exchange(jnp.where(up, top, low), jnp.where(up, low, top), pairs)
+    return rows
+
+
 def renormalise(weighted):
     return weighted / jnp.sqrt(jnp.sum(weighted * weighted, axis=1, keepdims=True) + 1e-06)
 
@@ -56,6 +69,7 @@
 
 
 PIECES = 2
+RING = (0, 3, 1, 2)
 
 
 def first_kernel(split, points, centroids, logits, local, xs, cs, ordered, xsem, csem):
@@ -75,7 +89,7 @@
             for z in range(nz):
                 for x in range(nx):
                     here = ((y * nz + z) * nx + x) * rows
-                    there = ((y * nx + x) * nz + z) * rows
+                    there = ((y * nx + x) * nz + RING.index(z)) * rows
                     ordered[there : there + rows, c] = cs[here : here + rows, c]
         chigh, clow = halves(ordered[:, c])
         xcopies[i].wait()
@@ -127,7 +141,7 @@
         if turn < ITERS - 1:
             mine = renormalise(jnp.sum(lax.all_gather(part, "zh"), axis=0))
             current = gather(mine, ("y", "x")).reshape(centroids.shape)
-    owned = renormalise(scatter_sum(part, ("zh",)))
+    owned = renormalise(ring_scatter(part))
     return owned[None], total
 
 

time: 133 us -> 136 us (1.023)
  blocking collectives: 123 us -> 86.4 us
  waiting for transfers between devices: 0 us -> 26.3 us
  starting transfers between devices: 0 us -> 11.5 us
    all_to_all x3 -> x1, blocking collectives: 57.4 us -> 20.7 us  [scatter_sum(): lax.all_to_all(blocks, axes, split_axis=0, concat_axis=0, tiled=True)]
    all_to_all x0 -> x1, waiting for transfers between devices: none -> 16.2 us  [scatter_sum(): lax.all_to_all(blocks, axes, split_axis=0, concat_axis=0, tiled=True)]
    ppermute x0 -> x2, waiting for transfers between devices: none -> 10.1 us  [exchange(): lax.ppermute(send, 'zh', [p for a, b in pairs for p in ((a, b), (b, a))])]
    ppermute x0 -> x2, starting transfers between devices: none -> 7.87 us  [exchange(): lax.ppermute(send, 'zh', [p for a, b in pairs for p in ((a, b), (b, a))])]
    all_to_all x0 -> x1, starting transfers between devices: none -> 3.65 us  [scatter_sum(): lax.all_to_all(blocks, axes, split_axis=0, concat_axis=0, tiled=True)]
  transfers between devices with their start and end apart: 0 -> 3, of which waited for: 0 -> 3; matrix products, arithmetic and copies ran while one was open for 0% -> 0% of each run, Pallas kernels for 0% -> 0%
where the time goes in v10:
time: 136 us; the launch traced here: 134 us
  blocking collectives  86.4 us (64%)
  waiting for transfers between devices  26.3 us (19%)
  starting transfers between devices  11.5 us (8%)
  matrix products  4.24 us (3%)
  Pallas kernels  2.99 us (2%)
  other arithmetic  1.43 us (1%)
    all_to_all x3, blocking collectives, gather(): return lax.all_to_all(copies, axes, split_axis=0, concat_axis=0, tiled=True)  43.2 us
    all_gather x1, blocking collectives, shards(): mine = renormalise(jnp.sum(lax.all_gather(part, 'zh'), axis=0))  22.5 us
    all_to_all x1, blocking collectives, scatter_sum(): lax.all_to_all(blocks, axes, split_axis=0, concat_axis=0, tiled=True)  20.7 us
    all_to_all x1, waiting for transfers between devices, scatter_sum(): lax.all_to_all(blocks, axes, split_axis=0, concat_axis=0, tiled=True)  16.2 us
    ppermute x2, waiting for transfers between devices, exchange(): lax.ppermute(send, 'zh', [p for a, b in pairs for p in ((a, b), (b, a))])  10.1 us
    ppermute x2, starting transfers between devices, exchange(): lax.ppermute(send, 'zh', [p for a, b in pairs for p in ((a, b), (b, a))])  7.87 us
    dot_general x3, matrix products, dot(): lax.dot_general(a, b, (dims, ((), ())), precision=lax.Precision.HIGH, pre...  4.24 us
    all_to_all x1, starting transfers between devices, scatter_sum(): lax.all_to_all(blocks, axes, split_axis=0, concat_axis=0, tiled=True)  3.65 us
  transfers between devices with their start and end apart: 3, of which 3 were waited for; matrix products, arithmetic and copies ran while one was open for 0% of the time, Pallas kernels for 0%

profile of v10, /device:TPU:1, one launch (start us, length us, event | category | flops | bytes accessed | tf_op | source)
XLA Modules:
  0.0 133.8 jit_solution(1024839633054787982)
XLA Ops:
  0.6 0.0 copy-start
  0.6 3.0 %shard_map.41 = (f32[256,512]{1,0:T(8,128)S(1)}, f32[1,512]{1,0:T(1,128)S(1)}) custom-call(f32[512,1024]{1,0:T(8,128)} %refs_0_.1, f32[256,1024]{1,0:T(8,128)} %refs_1_.1), custom_call_target="tpu_custom_call" | custom-call | tf_op jit(solution)/shard_map/pallas_call | solution.py:111
  3.7 14.2 %all_to_all.25 = f32[8,1,512]{2,1,0:T(1,128)S(1)} all-to-all(f32[8,1,512]{2,1,0:T(1,128)S(1)} %broadcast_in_dim.11), channel_id=1, replica_groups=mesh['y'=4,'zh'=4,'x'=4,'zl'=4,'core'=2] {'zl','core'}, dimensions={0} | all-to-all | bytes 32768 | tf_op jit(solution)/shard_map/all_to_all | solution.py:40
  17.9 0.0 copy-done
  17.9 1.1 fusion.3
  19.0 20.7 %all_to_all.26 = f32[16,16,1024]{2,1,0:T(8,128)S(1)} all-to-all(f32[16,16,1024]{2,1,0:T(8,128)S(1)} %bitcast.14), channel_id=1, replica_groups=mesh['y'=4,'zh'=4,'x'=4,'zl'=4,'core'=2] {'y','x'}, dimensions={0} | all-to-all | bytes 2097152 | tf_op jit(solution)/shard_map/all_to_all | solution.py:46
  39.7 0.1 reduce_sum.73
  39.8 22.5 %all-gather = f32[64,1024]{1,0:T(8,128)S(1)} all-gather(f32[16,1024]{1,0:T(8,128)S(1)} %reduce_sum.73), channel_id=2, replica_groups=mesh['y'=4,'zh'=4,'x'=4,'zl'=4,'core'=2] {'zh'}, dimensions={0}, use_global_device_ids=true | all-gather | bytes 327680 | tf_op jit(solution)/shard_map/all_gather | solution.py:142
  62.3 0.1 multiply_reduce_fusion
  62.4 0.1 broadcast_divide_fusion
  62.5 0.1 broadcast_in_dim.12
  62.6 14.9 %all_to_all.27 = f32[16,16,1024]{2,1,0:T(8,128)S(1)} all-to-all(f32[16,16,1024]{2,1,0:T(8,128)S(1)} %broadcast_in_dim.12), channel_id=1, replica_groups=mesh['y'=4,'zh'=4,'x'=4,'zl'=4,'core'=2] {'y','x'}, dimensions={0} | all-to-all | bytes 2097152 | tf_op jit(solution)/shard_map/all_to_all | solution.py:40
  77.4 1.1 fusion.12
  78.5 0.1 exponential_reduce_fusion
  78.7 14.2 %all_to_all.28 = f32[8,1,512]{2,1,0:T(1,128)S(1)} all-to-all(f32[8,1,512]{2,1,0:T(1,128)S(1)} %broadcast_in_dim.13), channel_id=1, replica_groups=mesh['y'=4,'zh'=4,'x'=4,'zl'=4,'core'=2] {'zl','core'}, dimensions={0} | all-to-all | bytes 32768 | tf_op jit(solution)/shard_map/all_to_all | solution.py:40
  92.9 0.0 copy-start.1
  92.9 2.1 %fusion = f32[256,1024]{1,0:T(8,128)} fusion(f32[512,1024]{1,0:T(8,128)S(1)} %copy-done, f32[256,512]{1,0:T(8,128)S(1)} %get-tuple-element.9, f32[512]{0:T(512)S(1)} %log_add_fusion), kind=kOutput, calls=%fused_computation.1 | convolution fusion | flops 805437440 | bytes 3672064 | tf_op jit(solution)/shard_map/dot_general | solution.py:16
  95.0 0.0 copy-done.1
  95.0 3.7 %all-to-all-start.4 = ((f32[16,16,1024]{2,1,0:T(8,128)}), f32[16,16,1024]{2,1,0:T(8,128)S(1)}, u32[]{:S(2)}, u32[]{:S(2)}) async-start(f32[16,16,1024]{2,1,0:T(8,128)} %bitcast.12), calls=%async_computation.4 | async-start | bytes 2097152 | tf_op jit(solution)/shard_map/all_to_all | solution.py:46
  98.7 16.2 %all-to-all-done.4 = f32[16,16,1024]{2,1,0:T(8,128)S(1)} async-done(((f32[16,16,1024]{2,1,0:T(8,128)}), f32[16,16,1024]{2,1,0:T(8,128)S(1)}, u32[]{:S(2)}, u32[]{:S(2)}) %all-to-all-start.4) | async-done | bytes 1048608 | tf_op jit(solution)/shard_map/all_to_all | solution.py:46
  114.9 0.1 reduce_sum.78
  114.9 4.4 %collective-permute-start = (f32[8,1024]{1,0:T(8,128)S(1)}, f32[8,1024]{1,0:T(8,128)S(1)}, u32[]{:S(2)}, u32[]{:S(2)}) collective-permute-start(f32[8,1024]{1,0:T(8,128)S(1)} %slice_select_fusion), channel_id=1, source_target_pairs={{0,32},{32,0},{64,96},{96,64},{1,33},{33,1},{65,97},{97,65},{2,34}... | collective-permute-start | bytes 98312 | tf_op jit(solution)/shard_map/ppermute | solution.py:50
  119.4 5.2 %collective-permute-done = f32[8,1024]{1,0:T(8,128)S(1)} collective-permute-done((f32[8,1024]{1,0:T(8,128)S(1)}, f32[8,1024]{1,0:T(8,128)S(1)}, u32[]{:S(2)}, u32[]{:S(2)}) %collective-permute-start) | collective-permute-done | bytes 32800 | tf_op jit(solution)/shard_map/ppermute | solution.py:50
  124.6 3.4 %collective-permute-start.1 = (f32[4,1024]{1,0:T(4,128)S(1)}, f32[4,1024]{1,0:T(4,128)S(1)}, u32[]{:S(2)}, u32[]{:S(2)}) collective-permute-start(f32[4,1024]{1,0:T(4,128)S(1)} %slice_select_fusion.1), channel_id=1, source_target_pairs={{32,64},{64,32},{96,0},{0,96},{33,65},{65,33},{97,1},{1,97},{34,66... | collective-permute-start | bytes 49160 | tf_op jit(solution)/shard_map/ppermute | solution.py:50
  128.0 4.9 %collective-permute-done.1 = f32[4,1024]{1,0:T(4,128)S(1)} collective-permute-done((f32[4,1024]{1,0:T(4,128)S(1)}, f32[4,1024]{1,0:T(4,128)S(1)}, u32[]{:S(2)}, u32[]{:S(2)}) %collective-permute-start.1) | collective-permute-done | bytes 16416 | tf_op jit(solution)/shard_map/ppermute | solution.py:50
  132.9 0.1 multiply_reduce_fusion.1
  133.1 0.7 divide_bitcast_fusion
  (15 shorter events, 0.2 us)
Async XLA Ops:
  0.6 17.3 %copy-start = (f32[512,1024]{1,0:T(8,128)S(1)}, f32[512,1024]{1,0:T(8,128)}, u32[]{:S(2)}) copy-start(f32[512,1024]{1,0:T(8,128)} %refs_0_.1) | copy-start | bytes 6291460
  92.9 2.1 %copy-start.1 = (f32[512]{0:T(512)}, f32[512]{0:T(512)S(1)}, u32[]{:S(2)}) copy-start(f32[512]{0:T(512)S(1)} %log_add_fusion) | copy-start | bytes 6148
  95.0 19.9 %all-to-all-start.4 = ((f32[16,16,1024]{2,1,0:T(8,128)}), f32[16,16,1024]{2,1,0:T(8,128)S(1)}, u32[]{:S(2)}, u32[]{:S(2)}) async-start(f32[16,16,1024]{2,1,0:T(8,128)} %bitcast.12), calls=%async_computation.4 | async-start | bytes 2097152 | tf_op jit(solution)/shard_map/all_to_all | solution.py:46
  114.9 9.6 %collective-permute-start = (f32[8,1024]{1,0:T(8,128)S(1)}, f32[8,1024]{1,0:T(8,128)S(1)}, u32[]{:S(2)}, u32[]{:S(2)}) collective-permute-start(f32[8,1024]{1,0:T(8,128)S(1)} %slice_select_fusion), channel_id=1, source_target_pairs={{0,32},{32,0},{64,96},{96,64},{1,33},{33,1},{65,97},{97,65},{2,34}... | collective-permute-start | bytes 98312 | tf_op jit(solution)/shard_map/ppermute | solution.py:50
  124.6 8.4 %collective-permute-start.1 = (f32[4,1024]{1,0:T(4,128)S(1)}, f32[4,1024]{1,0:T(4,128)S(1)}, u32[]{:S(2)}, u32[]{:S(2)}) collective-permute-start(f32[4,1024]{1,0:T(4,128)S(1)} %slice_select_fusion.1), channel_id=1, source_target_pairs={{32,64},{64,32},{96,0},{0,96},{33,65},{65,33},{97,1},{1,97},{34,66... | collective-permute-start | bytes 49160 | tf_op jit(solution)/shard_map/ppermute | solution.py:50

commit v11 on v9

--- a/solution.py
+++ b/solution.py
@@ -148,7 +148,9 @@
         if turn < ITERS - 1:
             mine = renormalise(jnp.sum(lax.all_gather(part, "zh"), axis=0))
             current = gather(mine, PLANE).reshape(centroids.shape)
-    owned = renormalise(scatter_sum(part, ("zh",)))
+    rows = part.shape[0] // lax.axis_size("zh")
+    blocks = lax.dynamic_slice_in_dim(lax.all_gather(part, "zh"), lax.axis_index("zh") * rows, rows, 1)
+    owned = renormalise(jnp.sum(blocks, axis=0))
     return owned[None], total
 
 

time: 133 us -> 137 us (1.030); the launches traced: 133 us -> 134 us
  blocking collectives: 124 us -> 105 us
  waiting for transfers between devices: 0 us -> 15.9 us
  starting transfers between devices: 0 us -> 3.65 us
    all_to_all x6 -> x4, blocking collectives: 102 us -> 64.2 us  [swap(): lax.all_to_all(blocks, axes, split_axis=0, concat_axis=0, tiled=True, axi...]
    all_gather x0 -> x1, blocking collectives: none -> 18.6 us  [shards(): lax.all_gather(part, 'zh')]
    all_to_all x0 -> x1, waiting for transfers between devices: none -> 15.9 us  [swap(): lax.all_to_all(blocks, axes, split_axis=0, concat_axis=0, tiled=True, axi...]
    all_to_all x0 -> x1, starting transfers between devices: none -> 3.65 us  [swap(): lax.all_to_all(blocks, axes, split_axis=0, concat_axis=0, tiled=True, axi...]
  transfers between devices with their start and end apart: 0 -> 1, of which waited for: 0 -> 1; matrix products, arithmetic and copies ran while one was open for 0% -> 0% of each run, Pallas kernels for 0% -> 0%
where the time goes in v11:
time: 137 us; the launch traced here: 134 us
  blocking collectives  105 us (77%)
  waiting for transfers between devices  15.9 us (12%)
  matrix products  4.24 us (3%)
  starting transfers between devices  3.65 us (3%)
  Pallas kernels  3 us (2%)
  other arithmetic  1.44 us (1%)
    all_to_all x4, blocking collectives, swap(): lax.all_to_all(blocks, axes, split_axis=0, concat_axis=0, tiled=True, axi...  64.2 us
    all_gather x1, blocking collectives, shards(): mine = renormalise(jnp.sum(lax.all_gather(part, 'zh'), axis=0))  22.2 us
    all_gather x1, blocking collectives, shards(): lax.all_gather(part, 'zh')  18.6 us
    all_to_all x1, waiting for transfers between devices, swap(): lax.all_to_all(blocks, axes, split_axis=0, concat_axis=0, tiled=True, axi...  15.9 us
    dot_general x3, matrix products, dot(): lax.dot_general(a, b, (dims, ((), ())), precision=lax.Precision.HIGH, pre...  4.24 us
    all_to_all x1, starting transfers between devices, swap(): lax.all_to_all(blocks, axes, split_axis=0, concat_axis=0, tiled=True, axi...  3.65 us
    pallas_call x1, Pallas kernels, first_logits(): pl.pallas_call(lambda *refs: first_kernel(split, *refs), out_shape=(jax.S...  3 us
  transfers between devices with their start and end apart: 1, of which 1 were waited for; matrix products, arithmetic and copies ran while one was open for 0% of the time, Pallas kernels for 0%

profile of v11, /device:TPU:1, one launch (start us, length us, event | category | flops | bytes accessed | tf_op | source)
XLA Modules:
  0.0 134.1 jit_solution(7934850348189211283)
XLA Ops:
  0.6 0.0 copy-start
  0.6 3.0 %shard_map.41 = (f32[256,512]{1,0:T(8,128)S(1)}, f32[1,512]{1,0:T(1,128)S(1)}) custom-call(f32[512,1024]{1,0:T(8,128)} %refs_0_.1, f32[256,1024]{1,0:T(8,128)} %refs_1_.1), custom_call_target="tpu_custom_call" | custom-call | tf_op jit(solution)/shard_map/pallas_call | solution.py:118
  3.7 14.2 %all_to_all.25 = f32[8,1,512]{2,1,0:T(1,128)S(1)} all-to-all(f32[8,1,512]{2,1,0:T(1,128)S(1)} %broadcast_in_dim.9), channel_id=1, replica_groups=mesh['y'=4,'zh'=4,'x'=4,'zl'=4,'core'=2] {'zl','core'}, dimensions={0} | all-to-all | bytes 32768 | tf_op jit(solution)/shard_map/all_to_all | solution.py:49
  17.9 0.0 copy-done
  17.9 1.1 fusion.3
  19.0 21.0 %all_to_all.26 = f32[16,16,1024]{2,1,0:T(8,128)S(1)} all-to-all(f32[16,16,1024]{2,1,0:T(8,128)S(1)} %bitcast.15), channel_id=1, replica_groups={{0,8,16,24,128,136,144,152,256,264,272,280,384,392,400,408},{1,129,257,..., dimensions={0} | all-to-all | bytes 2097152 | tf_op jit(solution)/shard_map/all_to_all | solution.py:49
  40.0 0.1 reduce_sum.84
  40.1 22.2 %all-gather = f32[64,1024]{1,0:T(8,128)S(1)} all-gather(f32[16,1024]{1,0:T(8,128)S(1)} %reduce_sum.84), channel_id=2, replica_groups=mesh['y'=4,'zh'=4,'x'=4,'zl'=4,'core'=2] {'zh'}, dimensions={0}, use_global_device_ids=true | all-gather | bytes 327680 | tf_op jit(solution)/shard_map/all_gather | solution.py:149
  62.2 0.1 multiply_reduce_fusion
  62.4 0.1 broadcast_divide_fusion
  62.5 0.1 broadcast_in_dim.10
  62.6 14.9 %all_to_all.27 = f32[16,16,1024]{2,1,0:T(8,128)S(1)} all-to-all(f32[16,16,1024]{2,1,0:T(8,128)S(1)} %broadcast_in_dim.10), channel_id=1, replica_groups={{0,8,16,24,128,136,144,152,256,264,272,280,384,392,400,408},{1,129,257,..., dimensions={0} | all-to-all | bytes 2097152 | tf_op jit(solution)/shard_map/all_to_all | solution.py:49
  77.5 1.1 fusion.12
  78.6 0.1 exponential_reduce_fusion
  78.8 14.1 %all_to_all.28 = f32[8,1,512]{2,1,0:T(1,128)S(1)} all-to-all(f32[8,1,512]{2,1,0:T(1,128)S(1)} %broadcast_in_dim.11), channel_id=1, replica_groups=mesh['y'=4,'zh'=4,'x'=4,'zl'=4,'core'=2] {'zl','core'}, dimensions={0} | all-to-all | bytes 32768 | tf_op jit(solution)/shard_map/all_to_all | solution.py:49
  93.0 0.0 copy-start.1
  93.0 2.1 %fusion = f32[256,1024]{1,0:T(8,128)} fusion(f32[512,1024]{1,0:T(8,128)S(1)} %copy-done, f32[256,512]{1,0:T(8,128)S(1)} %get-tuple-element.7, f32[512]{0:T(512)S(1)} %log_add_fusion), kind=kOutput, calls=%fused_computation.1 | convolution fusion | flops 805437440 | bytes 3672064 | tf_op jit(solution)/shard_map/dot_general | solution.py:19
  95.0 0.0 copy-done.1
  95.0 3.7 %all-to-all-start.4 = ((f32[16,16,1024]{2,1,0:T(8,128)}), f32[16,16,1024]{2,1,0:T(8,128)S(1)}, u32[]{:S(2)}, u32[]{:S(2)}) async-start(f32[16,16,1024]{2,1,0:T(8,128)} %bitcast.13), calls=%async_computation.4 | async-start | bytes 2097152 | tf_op jit(solution)/shard_map/all_to_all | solution.py:49
  98.7 15.9 %all-to-all-done.4 = f32[16,16,1024]{2,1,0:T(8,128)S(1)} async-done(((f32[16,16,1024]{2,1,0:T(8,128)}), f32[16,16,1024]{2,1,0:T(8,128)S(1)}, u32[]{:S(2)}, u32[]{:S(2)}) %all-to-all-start.4) | async-done | bytes 1048608 | tf_op jit(solution)/shard_map/all_to_all | solution.py:49
  114.6 0.1 reduce_sum.89
  114.6 18.6 %all-gather.1 = f32[64,1024]{1,0:T(8,128)S(1)} all-gather(f32[16,1024]{1,0:T(8,128)S(1)} %reduce_sum.89), channel_id=3, replica_groups=mesh['y'=4,'zh'=4,'x'=4,'zl'=4,'core'=2] {'zh'}, dimensions={0}, use_global_device_ids=true | all-gather | bytes 327680 | tf_op jit(solution)/shard_map/all_gather | solution.py:152
  133.3 0.1 multiply_reduce_fusion.1
  133.5 0.7 bitcast_divide_fusion
  (13 shorter events, 0.2 us)
Async XLA Ops:
  0.6 17.3 %copy-start = (f32[512,1024]{1,0:T(8,128)S(1)}, f32[512,1024]{1,0:T(8,128)}, u32[]{:S(2)}) copy-start(f32[512,1024]{1,0:T(8,128)} %refs_0_.1) | copy-start | bytes 6291460
  93.0 2.1 %copy-start.1 = (f32[512]{0:T(512)}, f32[512]{0:T(512)S(1)}, u32[]{:S(2)}) copy-start(f32[512]{0:T(512)S(1)} %log_add_fusion) | copy-start | bytes 6148
  95.0 19.5 %all-to-all-start.4 = ((f32[16,16,1024]{2,1,0:T(8,128)}), f32[16,16,1024]{2,1,0:T(8,128)S(1)}, u32[]{:S(2)}, u32[]{:S(2)}) async-start(f32[16,16,1024]{2,1,0:T(8,128)} %bitcast.13), calls=%async_computation.4 | async-start | bytes 2097152 | tf_op jit(solution)/shard_map/all_to_all | solution.py:49

commit v12 on v9

--- a/solution.py
+++ b/solution.py
@@ -140,14 +140,14 @@
     logits, local = first_logits(points, centroids, split)
     for turn in range(ITERS):
         if turn:
-            logits = dot(current, points, ((1,), (1,))) / TAU
+            logits = dot(current, points, ((1,), (1,)))
             local = lse(logits, 0)
         total = lse(gather(local, CEN), 0)[0, 0]
         weighted = dot(jnp.exp(logits - total[None]), points, ((1,), (0,)))
         part = scatter_sum(weighted, PLANE)
         if turn < ITERS - 1:
             mine = renormalise(jnp.sum(lax.all_gather(part, "zh"), axis=0))
-            current = gather(mine, PLANE).reshape(centroids.shape)
+            current = gather(mine / TAU, PLANE).reshape(centroids.shape)
     owned = renormalise(scatter_sum(part, ("zh",)))
     return owned[None], total
 

time: 133 us -> 133 us (level)
  no operation moved by 1% of the time
where the time goes in v12:
time: 133 us
  blocking collectives  124 us (93%)
  matrix products  3.25 us (2%)
  Pallas kernels  3 us (2%)
  other arithmetic  1.43 us (1%)
    all_to_all x6, blocking collectives, swap(): lax.all_to_all(blocks, axes, split_axis=0, concat_axis=0, tiled=True, axi...  102 us
    all_gather x1, blocking collectives, shards(): mine = renormalise(jnp.sum(lax.all_gather(part, 'zh'), axis=0))  22.2 us
    dot_general x3, matrix products, dot(): lax.dot_general(a, b, (dims, ((), ())), precision=lax.Precision.HIGH, pre...  3.25 us
    pallas_call x1, Pallas kernels, first_logits(): pl.pallas_call(lambda *refs: first_kernel(split, *refs), out_shape=(jax.S...  3 us

profile of v12, /device:TPU:1, one launch (start us, length us, event | category | flops | bytes accessed | tf_op | source)
XLA Modules:
  0.0 132.8 jit_solution(17216680675023741745)
XLA Ops:
  0.6 0.0 copy-start
  0.6 3.0 %shard_map.41 = (f32[256,512]{1,0:T(8,128)S(1)}, f32[1,512]{1,0:T(1,128)S(1)}) custom-call(f32[512,1024]{1,0:T(8,128)} %refs_0_.1, f32[256,1024]{1,0:T(8,128)} %refs_1_.1), custom_call_target="tpu_custom_call" | custom-call | tf_op jit(solution)/shard_map/pallas_call | solution.py:118
  3.7 14.2 %all_to_all.30 = f32[8,1,512]{2,1,0:T(1,128)S(1)} all-to-all(f32[8,1,512]{2,1,0:T(1,128)S(1)} %broadcast_in_dim.9), channel_id=1, replica_groups=mesh['y'=4,'zh'=4,'x'=4,'zl'=4,'core'=2] {'zl','core'}, dimensions={0} | all-to-all | bytes 32768 | tf_op jit(solution)/shard_map/all_to_all | solution.py:49
  17.9 0.0 copy-done
  17.9 1.1 fusion.3
  19.0 21.0 %all_to_all.31 = f32[16,16,1024]{2,1,0:T(8,128)S(1)} all-to-all(f32[16,16,1024]{2,1,0:T(8,128)S(1)} %bitcast.13), channel_id=1, replica_groups={{0,8,16,24,128,136,144,152,256,264,272,280,384,392,400,408},{1,129,257,..., dimensions={0} | all-to-all | bytes 2097152 | tf_op jit(solution)/shard_map/all_to_all | solution.py:49
  40.0 0.1 reduce_sum.84
  40.1 22.2 %all-gather = f32[64,1024]{1,0:T(8,128)S(1)} all-gather(f32[16,1024]{1,0:T(8,128)S(1)} %reduce_sum.84), channel_id=2, replica_groups=mesh['y'=4,'zh'=4,'x'=4,'zl'=4,'core'=2] {'zh'}, dimensions={0}, use_global_device_ids=true | all-gather | bytes 327680 | tf_op jit(solution)/shard_map/all_gather | solution.py:149
  62.2 0.1 multiply_reduce_fusion
  62.4 0.1 divide_multiply_fusion
  62.5 0.1 broadcast_in_dim.10
  62.6 14.9 %all_to_all.32 = f32[16,16,1024]{2,1,0:T(8,128)S(1)} all-to-all(f32[16,16,1024]{2,1,0:T(8,128)S(1)} %broadcast_in_dim.10), channel_id=1, replica_groups={{0,8,16,24,128,136,144,152,256,264,272,280,384,392,400,408},{1,129,257,..., dimensions={0} | all-to-all | bytes 2097152 | tf_op jit(solution)/shard_map/all_to_all | solution.py:49
  77.5 1.1 fusion.12
  78.6 0.1 exponential_reduce_fusion
  78.8 14.1 %all_to_all.33 = f32[8,1,512]{2,1,0:T(1,128)S(1)} all-to-all(f32[8,1,512]{2,1,0:T(1,128)S(1)} %broadcast_in_dim.11), channel_id=1, replica_groups=mesh['y'=4,'zh'=4,'x'=4,'zl'=4,'core'=2] {'zl','core'}, dimensions={0} | all-to-all | bytes 32768 | tf_op jit(solution)/shard_map/all_to_all | solution.py:49
  93.0 0.0 copy-start.1
  93.0 1.1 fusion
  94.1 19.1 %all_to_all.34 = f32[16,16,1024]{2,1,0:T(8,128)S(1)} all-to-all(f32[16,16,1024]{2,1,0:T(8,128)S(1)} %bitcast.14), channel_id=1, replica_groups={{0,8,16,24,128,136,144,152,256,264,272,280,384,392,400,408},{1,129,257,..., dimensions={0} | all-to-all | bytes 2097152 | tf_op jit(solution)/shard_map/all_to_all | solution.py:49
  113.2 0.0 copy-done.1
  113.2 0.1 reduce_sum.89
  113.3 18.6 %all_to_all.35 = f32[4,4,1024]{2,1,0:T(4,128)S(1)} all-to-all(f32[4,4,1024]{2,1,0:T(4,128)S(1)} %reshape.125), channel_id=1, replica_groups=mesh['y'=4,'zh'=4,'x'=4,'zl'=4,'core'=2] {'zh'}, dimensions={0} | all-to-all | bytes 131072 | tf_op jit(solution)/shard_map/all_to_all | solution.py:49
  131.9 0.1 multiply_reduce_fusion.1
  132.1 0.7 bitcast_divide_fusion
  (14 shorter events, 0.2 us)
Async XLA Ops:
  0.6 17.3 %copy-start = (f32[512,1024]{1,0:T(8,128)S(1)}, f32[512,1024]{1,0:T(8,128)}, u32[]{:S(2)}) copy-start(f32[512,1024]{1,0:T(8,128)} %refs_0_.1) | copy-start | bytes 6291460
  93.0 20.2 %copy-start.1 = (f32[512]{0:T(512)}, f32[512]{0:T(512)S(1)}, u32[]{:S(2)}) copy-start(f32[512]{0:T(512)S(1)} %log_add_fusion) | copy-start | bytes 6148

commit v13 on v9

--- a/solution.py
+++ b/solution.py
@@ -142,7 +142,7 @@
         if turn:
             logits = dot(current, points, ((1,), (1,))) / TAU
             local = lse(logits, 0)
-        total = lse(gather(local, CEN), 0)[0, 0]
+        total = lse(gather(local, CEN[::-1]), 0)[0, 0]
         weighted = dot(jnp.exp(logits - total[None]), points, ((1,), (0,)))
         part = scatter_sum(weighted, PLANE)
         if turn < ITERS - 1:

time: 133 us -> 134 us (level)
  no operation moved by 1% of the time
where the time goes in v13:
time: 134 us; the launch traced here: 133 us
  blocking collectives  125 us (93%)
  matrix products  3.25 us (2%)
  Pallas kernels  3 us (2%)
  other arithmetic  1.43 us (1%)
    all_to_all x6, blocking collectives, swap(): lax.all_to_all(blocks, axes, split_axis=0, concat_axis=0, tiled=True, axi...  102 us
    all_gather x1, blocking collectives, shards(): mine = renormalise(jnp.sum(lax.all_gather(part, 'zh'), axis=0))  22.6 us
    dot_general x3, matrix products, dot(): lax.dot_general(a, b, (dims, ((), ())), precision=lax.Precision.HIGH, pre...  3.25 us
    pallas_call x1, Pallas kernels, first_logits(): pl.pallas_call(lambda *refs: first_kernel(split, *refs), out_shape=(jax.S...  3 us

profile of v13, /device:TPU:1, one launch (start us, length us, event | category | flops | bytes accessed | tf_op | source)
XLA Modules:
  0.0 133.2 jit_solution(15908105150208841465)
XLA Ops:
  0.6 0.0 copy-start
  0.6 3.0 %shard_map.41 = (f32[256,512]{1,0:T(8,128)S(1)}, f32[1,512]{1,0:T(1,128)S(1)}) custom-call(f32[512,1024]{1,0:T(8,128)} %refs_0_.1, f32[256,1024]{1,0:T(8,128)} %refs_1_.1), custom_call_target="tpu_custom_call" | custom-call | tf_op jit(solution)/shard_map/pallas_call | solution.py:118
  3.7 14.5 %all_to_all.30 = f32[8,1,512]{2,1,0:T(1,128)S(1)} all-to-all(f32[8,1,512]{2,1,0:T(1,128)S(1)} %broadcast_in_dim.9), channel_id=1, replica_groups=mesh['y'=4,'zh'=4,'x'=4,'zl'=4,'core'=2] {'core','zl'}, dimensions={0} | all-to-all | bytes 32768 | tf_op jit(solution)/shard_map/all_to_all | solution.py:49
  18.3 0.0 copy-done
  18.3 1.1 fusion.3
  19.4 21.1 %all_to_all.31 = f32[16,16,1024]{2,1,0:T(8,128)S(1)} all-to-all(f32[16,16,1024]{2,1,0:T(8,128)S(1)} %bitcast.13), channel_id=1, replica_groups={{0,8,16,24,128,136,144,152,256,264,272,280,384,392,400,408},{1,129,257,..., dimensions={0} | all-to-all | bytes 2097152 | tf_op jit(solution)/shard_map/all_to_all | solution.py:49
  40.4 0.1 reduce_sum.84
  40.5 22.6 %all-gather = f32[64,1024]{1,0:T(8,128)S(1)} all-gather(f32[16,1024]{1,0:T(8,128)S(1)} %reduce_sum.84), channel_id=2, replica_groups=mesh['y'=4,'zh'=4,'x'=4,'zl'=4,'core'=2] {'zh'}, dimensions={0}, use_global_device_ids=true | all-gather | bytes 327680 | tf_op jit(solution)/shard_map/all_gather | solution.py:149
  63.1 0.1 multiply_reduce_fusion
  63.2 0.1 broadcast_divide_fusion
  63.3 0.1 broadcast_in_dim.10
  63.4 14.7 %all_to_all.32 = f32[16,16,1024]{2,1,0:T(8,128)S(1)} all-to-all(f32[16,16,1024]{2,1,0:T(8,128)S(1)} %broadcast_in_dim.10), channel_id=1, replica_groups={{0,8,16,24,128,136,144,152,256,264,272,280,384,392,400,408},{1,129,257,..., dimensions={0} | all-to-all | bytes 2097152 | tf_op jit(solution)/shard_map/all_to_all | solution.py:49
  78.1 1.1 fusion.12
  79.2 0.1 exponential_reduce_fusion
  79.3 14.6 %all_to_all.33 = f32[8,1,512]{2,1,0:T(1,128)S(1)} all-to-all(f32[8,1,512]{2,1,0:T(1,128)S(1)} %broadcast_in_dim.11), channel_id=1, replica_groups=mesh['y'=4,'zh'=4,'x'=4,'zl'=4,'core'=2] {'core','zl'}, dimensions={0} | all-to-all | bytes 32768 | tf_op jit(solution)/shard_map/all_to_all | solution.py:49
  94.0 0.0 copy-start.1
  94.1 1.1 fusion
  95.1 19.2 %all_to_all.34 = f32[16,16,1024]{2,1,0:T(8,128)S(1)} all-to-all(f32[16,16,1024]{2,1,0:T(8,128)S(1)} %bitcast.14), channel_id=1, replica_groups={{0,8,16,24,128,136,144,152,256,264,272,280,384,392,400,408},{1,129,257,..., dimensions={0} | all-to-all | bytes 2097152 | tf_op jit(solution)/shard_map/all_to_all | solution.py:49
  114.4 0.0 copy-done.1
  114.4 0.1 reduce_sum.89
  114.5 17.9 %all_to_all.35 = f32[4,4,1024]{2,1,0:T(4,128)S(1)} all-to-all(f32[4,4,1024]{2,1,0:T(4,128)S(1)} %reshape.124), channel_id=1, replica_groups=mesh['y'=4,'zh'=4,'x'=4,'zl'=4,'core'=2] {'zh'}, dimensions={0} | all-to-all | bytes 131072 | tf_op jit(solution)/shard_map/all_to_all | solution.py:49
  132.3 0.1 multiply_reduce_fusion.1
  132.5 0.7 bitcast_divide_fusion
  (14 shorter events, 0.2 us)
Async XLA Ops:
  0.6 17.6 %copy-start = (f32[512,1024]{1,0:T(8,128)S(1)}, f32[512,1024]{1,0:T(8,128)}, u32[]{:S(2)}) copy-start(f32[512,1024]{1,0:T(8,128)} %refs_0_.1) | copy-start | bytes 6291460
  94.0 20.3 %copy-start.1 = (f32[512]{0:T(512)}, f32[512]{0:T(512)S(1)}, u32[]{:S(2)}) copy-start(f32[512]{0:T(512)S(1)} %log_add_fusion) | copy-start | bytes 6148
